TPU v7x, 512 devices: a whole 4x8x8 slice. The times are simulated.
512 devices in a mesh: vis: 8 (over z), ctx: 32 (over x, y), tp: 2 (over core).
Axes of the slice: x: 4, y: 8, z: 8, core: 2. Of those that a mesh axis runs over, the one named last changes fastest.
Arguments:
- patch_rows: bfloat16 [4096, 1280], P('ctx'), may hold values from -6 to 6
- vit_gain: float32 [1280], replicated, may hold values from 0.25 to 1.75
- vit_bias: float32 [1280], replicated, may hold values from -3 to 3
- vit_qkv: bfloat16 [1280, 3, 16, 80], P(None, None, ('vis', 'tp')), as said below
- vit_out: bfloat16 [16, 80, 1280], P(('vis', 'tp')), may hold values from -0.15625 to 0.15625
- merge_gain: float32 [1280], replicated, may hold values from 0.25 to 1.75
- merge_bias: float32 [1280], replicated, may hold values from -3 to 3
- merge_weight: bfloat16 [5120, 4096], P('ctx', ('vis', 'tp')), may hold values from -0.078125 to 0.078125
- image_patches: int32 [32, 2], replicated, may hold values from 4 to 64, as said below
- window_ids: int32 [4096], P('ctx'), may hold values from 0 to 4095, as said below
- image_pos: int32 [1024], replicated, may hold values from 0 to 4095, as said below
- slice_order: int32 [32], replicated, may hold values from 0 to 31, as said below
- doc_ids: int32 [4096], replicated, may hold values from 0 to 15, never falling along the last dimension, each value on 1 to 512 neighbouring positions
- text_rows: bfloat16 [4096, 4096], P('ctx', ('vis', 'tp')), may hold values from -6 to 6
- norm_gain: float32 [4096], replicated, may hold values from 0.25 to 1.75
- w_query: bfloat16 [4096, 8, 4, 128], P(None, 'vis', 'tp'), as said below
- w_keyval: bfloat16 [2, 4096, 8, 128], P('tp', None, 'vis'), as said below
Outputs:
- attention_out: bfloat16 [4096, 8, 512], P('ctx', 'vis', 'tp')
Inputs may be any that keep to these rules, and one draw needn't show every extreme that they name: `image_patches`: each is h * w for an image of h by w patches, h and w even and at most 32; the images of one ctx shard hold at most 128 patches together, exactly 128 on some shard. `window_ids`: equal ids mark one attention window: consecutive slots of one ctx shard, a multiple of 4 of them and at most 64, never in two images; slots after a shard's live patches form windows of 4. `slice_order`: a permutation; ctx shard c holds the sequence slices slice_order[c] and 63 - slice_order[c] of 64 positions, in that order, as its 128 rows. `image_pos`: distinct positions, one for every merged slot, live or not; the 32 slots of any one ctx shard put exactly 1 positions into the rows of each ctx shard. `doc_ids`: never falling along positions; each document holds 1 to 512 positions. `vit_qkv`: independent centred entries. `w_query`: independent centred entries. `w_keyval`: independent centred entries.
All inputs are finite; a program needn't handle non-finite values.
Results may differ from a plain program's by a relative error of at most 0.022.
The roundings to bfloat16 on the way count: a program that leaves them out, or rounds other values in their place, can miss the bound.
Values may be sent and summed in bfloat16 or wider, within the bound.
A program may use at most 64 MiB of HBM per device.

v0:
```python
import math

import jax
import jax.numpy as jnp
from jax import lax
from jax.sharding import PartitionSpec as P

D = 4096
HD = 128
VD = 1280
VHD = 80
TOK = 128
PCAP = 128
ICAP = 32


norm_eps = 1e-06
rope_base = 1000000.0
big_negative = -1e30


def swapped(value, axis, stride):
    return lax.ppermute(value, axis, [(i, i ^ 1 << stride) for i in range(lax.axis_size(axis))])


def layer_norm(values, scale_vec, shift_vec):
    centre = jnp.mean(values, axis=-1, keepdims=True)
    offset = values - centre
    spread = jnp.mean(offset * offset, axis=-1, keepdims=True)
    return offset * lax.rsqrt(spread + norm_eps) * scale_vec + shift_vec


def rotate(values, positions):
    half_dim = values.shape[-1] // 2
    exponent = jnp.arange(half_dim, dtype=jnp.float32) * (-2.0 / values.shape[-1])
    frequency = jnp.power(jnp.float32(rope_base), exponent)
    angles = positions.astype(jnp.float32)[:, None] * frequency[None, :]
    shape_out = (values.shape[0],) + (1,) * (values.ndim - 2) + (half_dim,)
    cosine = jnp.cos(angles).reshape(shape_out)
    sine_part = jnp.sin(angles).reshape(shape_out)
    lead_half = values[..., :half_dim]
    tail_half = values[..., half_dim:]
    return jnp.concatenate(
        [lead_half * cosine - tail_half * sine_part, tail_half * cosine + lead_half * sine_part],
        axis=-1,
    )


def row_positions(row_ids, slice_order, tokens_dev):
    shards = slice_order.shape[0]
    device_of = row_ids // tokens_dev
    local_row = row_ids % tokens_dev
    half_tok = tokens_dev // 2
    matches = device_of[:, None] == jnp.arange(shards, dtype=jnp.int32)[None, :]
    first_slice = jnp.sum(jnp.where(matches, slice_order[None, :], 0), axis=1)
    slice_ids = jnp.where(local_row < half_tok, first_slice, 2 * shards - 1 - first_slice)
    return slice_ids * half_tok + local_row % half_tok


def place_of(positions, slice_order, tokens_dev):
    shards = slice_order.shape[0]
    half_tok = tokens_dev // 2
    slice_ids = positions // half_tok
    paired = jnp.minimum(slice_ids, 2 * shards - 1 - slice_ids)
    owner_hot = (paired[..., None] == slice_order).astype(jnp.int32)
    owner_dev = jnp.sum(owner_hot * jnp.arange(shards, dtype=jnp.int32), axis=-1)
    local_row = jnp.where(slice_ids < shards, 0, half_tok) + positions % half_tok
    return (owner_dev, local_row, owner_hot)


def local(
    patch_rows,
    vit_gain,
    vit_bias,
    vit_qkv,
    vit_out,
    merge_gain,
    merge_bias,
    merge_weight,
    image_patches,
    window_ids,
    image_pos,
    slice_order,
    doc_ids,
    text_rows,
    norm_gain,
    w_query,
    w_keyval,
):
    shards = lax.axis_size("ctx")
    ctx_index = lax.axis_index("ctx")
    tp_index = lax.axis_index("tp")
    vit_heads = vit_qkv.shape[2]
    slab_width = merge_weight.shape[1]
    normed = layer_norm(patch_rows.astype(jnp.float32), vit_gain, vit_bias).astype(jnp.bfloat16)
    projected = jnp.dot(
        normed, vit_qkv.reshape(VD, 3 * vit_heads * VHD), preferred_element_type=jnp.float32
    )
    projected = projected.astype(jnp.bfloat16).reshape(PCAP, 3, vit_heads, VHD)
    scores = jnp.einsum(
        "qhd,khd->hqk", projected[:, 0], projected[:, 1], preferred_element_type=jnp.float32
    ) / math.sqrt(VHD)
    allowed = window_ids[:, None] == window_ids[None, :]
    scores = jnp.where(allowed[None], scores, big_negative)
    powers = jnp.exp(scores - jnp.max(scores, axis=-1, keepdims=True))
    totals = jnp.sum(powers, axis=-1)
    blended = jnp.einsum(
        "hqk,khd->qhd",
        powers.astype(jnp.bfloat16),
        projected[:, 2],
        preferred_element_type=jnp.float32,
    )
    blended = (
        (blended / jnp.transpose(totals)[:, :, None])
        .astype(jnp.bfloat16)
        .reshape(PCAP, vit_heads * VHD)
    )
    out_flat = vit_out.reshape(vit_heads * VHD, VD)
    branch_part = jnp.dot(blended, out_flat, preferred_element_type=jnp.float32)
    branch_sum = lax.psum(branch_part, ("vis", "tp"))
    hidden = patch_rows.astype(jnp.float32) + branch_sum
    merged = layer_norm(hidden, merge_gain, merge_bias).astype(jnp.bfloat16).reshape(ICAP, 4 * VD)
    image_emb = jnp.dot(
        merged,
        lax.all_gather(merge_weight, "ctx", axis=0, tiled=True),
        preferred_element_type=jnp.float32,
    ).astype(jnp.bfloat16)
    send_each = ICAP // shards
    slot_ids = jnp.arange(ICAP, dtype=jnp.int32)
    shard_ids = jnp.arange(shards, dtype=jnp.int32)
    live_count = jnp.sum(image_patches, axis=1) // 4
    all_pos = image_pos.reshape(shards, ICAP)
    owner_dev, local_row, owner_hot = place_of(all_pos, slice_order, TOK)
    before = jnp.cumsum(owner_hot, axis=1) - owner_hot
    rank_in = jnp.sum(before * owner_hot, axis=-1)
    is_live = slot_ids[None, :] < live_count[:, None]
    own_hot = (shard_ids == ctx_index)[:, None]
    own_owner = jnp.sum(jnp.where(own_hot, owner_dev, 0), axis=0)
    own_rank = jnp.sum(jnp.where(own_hot, rank_in, 0), axis=0)
    own_live = jnp.any(own_hot & is_live, axis=0)
    target_slot = own_owner * send_each + own_rank
    picker = ((target_slot[None, :] == slot_ids[:, None]) & own_live[None, :]).astype(jnp.bfloat16)
    outgoing = jnp.dot(picker, image_emb, preferred_element_type=jnp.float32).astype(jnp.bfloat16)
    incoming = lax.all_to_all(
        outgoing.reshape(shards, send_each, slab_width),
        "ctx",
        split_axis=0,
        concat_axis=0,
        tiled=True,
    )
    mine_live = ((owner_dev == ctx_index) & is_live).reshape(-1)
    column_of = (shard_ids[:, None] * send_each + rank_in).reshape(-1)
    row_hot = (
        (local_row.reshape(-1)[None, :] == jnp.arange(TOK, dtype=jnp.int32)[:, None])
        & mine_live[None, :]
    ).astype(jnp.bfloat16)
    column_hot = (column_of[:, None] == slot_ids[None, :]).astype(jnp.bfloat16)
    placing = jnp.dot(row_hot, column_hot, preferred_element_type=jnp.float32)
    is_image = jnp.sum(placing, axis=1) > 0.5
    image_part = jnp.dot(
        placing.astype(jnp.bfloat16),
        incoming.reshape(ICAP, slab_width),
        preferred_element_type=jnp.float32,
    )
    embeds = jnp.where(is_image[:, None], image_part.astype(jnp.bfloat16), text_rows)
    full_rows = lax.all_gather(embeds, ("vis", "tp"), axis=1, tiled=True)
    widened = full_rows.astype(jnp.float32)
    normed_rows = (
        widened
        * lax.rsqrt(jnp.mean(widened * widened, axis=1, keepdims=True) + norm_eps)
        * norm_gain
    ).astype(jnp.bfloat16)
    own_positions = row_positions(
        ctx_index * TOK + jnp.arange(TOK, dtype=jnp.int32), slice_order, TOK
    )
    own_doc = jnp.take(doc_ids, own_positions)
    kv_heads = w_query.shape[1]
    groups = w_query.shape[2]
    queries = jnp.dot(
        normed_rows, w_query.reshape(D, kv_heads * groups * HD), preferred_element_type=jnp.float32
    ).reshape(TOK, kv_heads, groups, HD)
    queries = rotate(queries, own_positions).astype(jnp.bfloat16)
    projected_half = jnp.dot(
        normed_rows, w_keyval[0].reshape(D, kv_heads * HD), preferred_element_type=jnp.float32
    ).reshape(TOK, kv_heads, HD)
    own_half = jnp.where(
        tp_index == 0, rotate(projected_half, own_positions), projected_half
    ).astype(jnp.bfloat16)
    initial = (
        jnp.full((kv_heads, groups, TOK), big_negative, jnp.float32),
        jnp.zeros((kv_heads, groups, TOK), jnp.float32),
        jnp.zeros((kv_heads, groups, TOK, HD), jnp.float32),
    )
    partner = swapped(own_half, "tp", 0)
    keys_here = jnp.where(tp_index == 0, own_half, partner)
    values_here = jnp.where(tp_index == 0, partner, own_half)
    carry_state = initial
    key_rows = lax.all_gather(keys_here, "ctx", axis=0, tiled=True)
    value_rows = lax.all_gather(values_here, "ctx", axis=0, tiled=True)
    key_count = key_rows.shape[0]
    block_rows = math.gcd(key_count, 1024)
    block_count = key_count // block_rows
    key_pos = row_positions(jnp.arange(key_count, dtype=jnp.int32), slice_order, TOK)
    key_doc = jnp.take(doc_ids, key_pos)
    stacked = (
        key_rows.reshape(block_count, block_rows, kv_heads, HD),
        value_rows.reshape(block_count, block_rows, kv_heads, HD),
        key_pos.reshape(block_count, block_rows),
        key_doc.reshape(block_count, block_rows),
    )

    def key_block(state_now, inputs_now):
        keys_blk, values_blk, pos_blk, doc_blk = inputs_now
        best_old, total_old, accum_old = state_now
        allowed_now = (pos_blk[None, :] <= own_positions[:, None]) & (
            doc_blk[None, :] == own_doc[:, None]
        )
        scores_now = jnp.einsum(
            "qkgd,nkd->kgqn", queries, keys_blk, preferred_element_type=jnp.float32
        ) / math.sqrt(HD)
        scores_now = jnp.where(allowed_now[None, None], scores_now, big_negative)
        best_new = jnp.maximum(best_old, jnp.max(scores_now, axis=-1))
        factor = jnp.exp(best_old - best_new)
        powers_now = jnp.where(
            allowed_now[None, None], jnp.exp(scores_now - best_new[..., None]), 0.0
        )
        total_new = total_old * factor + jnp.sum(powers_now, axis=-1)
        accum_new = accum_old * factor[..., None] + jnp.einsum(
            "kgqn,nkd->kgqd",
            powers_now.astype(jnp.bfloat16),
            values_blk,
            preferred_element_type=jnp.float32,
        )
        return ((best_new, total_new, accum_new), None)

    carry_state, unused = lax.scan(key_block, carry_state, stacked)
    best_final, total_final, accum_final = carry_state
    result = accum_final / total_final[..., None]
    return (
        jnp.transpose(result, (2, 0, 1, 3)).reshape(TOK, kv_heads, groups * HD).astype(jnp.bfloat16)
    )


def solution(mesh):
    placed = (
        P("ctx", None),
        P(),
        P(),
        P(None, None, ("vis", "tp"), None),
        P(("vis", "tp"), None, None),
        P(),
        P(),
        P("ctx", ("vis", "tp")),
        P(),
        P("ctx"),
        P(),
        P(),
        P(),
        P("ctx", ("vis", "tp")),
        P(),
        P(None, "vis", "tp", None),
        P("tp", None, "vis", None),
    )
    return jax.shard_map(
        local, mesh=mesh, in_specs=placed, out_specs=P("ctx", "vis", "tp"), check_vma=False
    )
```

profile of v0, /device:TPU:1, one launch (start us, length us, event | category | flops | bytes accessed | tf_op | source)
XLA Modules:
  0.0 375.7 jit_solution(1498065879978180166)
XLA Ops:
  7.4 1.2 convert_reduce_fusion
  8.6 1.2 fusion.34
  9.9 1.7 convolution_convert_fusion.1
  11.6 0.2 fusion.112
  11.9 1.3 fusion.38
  13.2 0.5 all-gather.5.cloned.1.call-update
  14.0 0.8 fusion.39
  15.1 1.0 fusion.110
  16.4 0.5 fusion.111
  16.9 119.6 %all-reduce.2.cloned.1.call-done = f32[128,1280]{1,0:T(8,128)} async-done(((f32[128,1280]{1,0:T(8,128)}), f32[128,1280]{1,0:T(8,128)}) %all-reduce.2.cloned.1.call-update) | async-done | bytes 655376 | tf_op jit(solution)/shard_map/psum | solution.py:120
  136.5 1.3 fusion.55
  137.8 1.3 multiply_reduce_fusion
  139.6 2.4 fusion.24
  142.1 0.5 broadcast.895
  142.6 0.7 reduce.6
  143.2 0.6 reshape.793
  143.9 8.6 %all-to-all-start = ((bf16[32,2,128]{2,1,0:T(2,128)(2,1)}), bf16[32,2,128]{2,1,0:T(2,128)(2,1)S(1)}, u32[]{:S(2)}, u32[]{:S(2)}) async-start(bf16[32,2,128]{2,1,0:T(2,128)(2,1)} %reshape.793), calls=%async_computation | async-start | bytes 32768 | tf_op jit(solution)/shard_map/all_to_all | solution.py:144
  152.6 8.5 %all-to-all-done = bf16[32,2,128]{2,1,0:T(2,128)(2,1)S(1)} async-done(((bf16[32,2,128]{2,1,0:T(2,128)(2,1)}), bf16[32,2,128]{2,1,0:T(2,128)(2,1)S(1)}, u32[]{:S(2)}, u32[]{:S(2)}) %all-to-all-start) | async-done | bytes 16416 | tf_op jit(solution)/shard_map/all_to_all | solution.py:144
  161.1 0.8 fusion.22
  162.2 36.3 %all-gather.7.cloned.1.call-done = bf16[128,4096]{1,0:T(8,128)(2,1)} async-done(((bf16[128,256]{1,0:T(8,128)(2,1)}), bf16[128,4096]{1,0:T(8,128)(2,1)}) %all-gather.7.cloned.1.call-update) | async-done | bytes 1048592 | tf_op jit(solution)/shard_map/all_gather | solution.py:166
  198.4 1.5 fusion.19
  200.0 1.8 fusion.29
  202.1 2.2 collective-permute-start
  204.3 0.9 collective-permute-done
  205.2 0.6 broadcast_select_fusion.1
  205.9 1.9 copy.82
  207.8 2.9 copy.65
  210.9 1.1 gather_fusion.1
  212.2 23.0 %gather_fusion = s32[4096]{0:T(1024)S(1)} fusion(s32[4096]{0:T(1024)S(1)} %copy-done.1, s32[4096]{0:T(1024)S(1)} %broadcast_clamp_fusion), kind=kCustom, calls=%fused_computation | custom fusion | bytes 49152 | tf_op jit(solution)/shard_map/jit(_take)/gather | solution.py:204
  235.5 2.0 convolution_bitcast_fusion.1
  237.7 38.7 %all-gather.9.cloned.1.call-done = bf16[4096,1,128]{0,2,1:T(8,128)(2,1)} async-done(((bf16[128,1,128]{0,2,1:T(8,128)(2,1)}), bf16[4096,1,128]{0,2,1:T(8,128)(2,1)}) %all-gather.9.cloned.1.call-update) | async-done | bytes 1048592 | tf_op jit(solution)/shard_map/all_gather | solution.py:198
  276.4 1.6 copy.71
  278.0 77.6 %all-gather.11.cloned.1.call-done = bf16[4096,1,128]{0,2,1:T(8,128)(2,1)} async-done(((bf16[128,1,128]{0,2,1:T(8,128)(2,1)}), bf16[4096,1,128]{0,2,1:T(8,128)(2,1)}) %all-gather.11.cloned.1.call-update) | async-done | bytes 1048592 | tf_op jit(solution)/shard_map/all_gather | solution.py:199
  355.6 2.3 copy.72
  357.8 9.5 %while.15 = (s32[]{:T(128)}, f32[1,2,128]{2,1,0:T(2,128)S(1)}, f32[1,2,128]{2,1,0:T(2,128)S(1)}, f32[1,2,128,128]{3,2,1,0:T(8,128)S(1)}, s32[4,1024]{1,0:T(4,128...) while((s32[]{:T(128)}, f32[1,2,128]{2,1,0:T(2,128)S(1)}, ...), condition=%wide.region_21.22_spmd.clone, body=%wide.region_18.21_spmd.clone.sunk | while | flops 137070080 | bytes 4564625 | solution.py:236
  357.9 0.3 compare_and_fusion.2
  358.2 0.3 fusion.127
  358.6 1.4 fusion.130
  360.2 0.3 compare_and_fusion.2
  360.6 0.3 fusion.127
  361.0 1.4 fusion.130
  362.6 0.3 compare_and_fusion.2
  363.0 0.3 fusion.127
  363.3 1.4 fusion.130
  365.0 0.3 compare_and_fusion.2
  365.3 0.3 fusion.127
  365.7 1.4 fusion.130
  367.4 0.7 copy_bitcast_fusion
  (105 shorter events, 3.7 us)
Async XLA Ops:
  7.4 192.6 %copy-start = (bf16[1,4096,1,128]{3,1,2,0:T(8,128)(2,1)S(1)}, bf16[1,4096,1,128]{3,1,2,0:T(8,128)(2,1)}, u32[]{:S(2)}) copy-start(bf16[1,4096,1,128]{3,1,2,0:T(8,128)(2,1)} %param.35) | copy-start | bytes 3145732
  7.4 4.2 %copy-start.13 = (s32[128]{0:T(128)S(1)}, s32[128]{0:T(128)}, u32[]{:S(2)}) copy-start(s32[128]{0:T(128)} %param.28) | copy-start | bytes 1540
  7.4 4.5 %copy-start.5 = (bf16[1,80,1280]{2,1,0:T(8,128)(2,1)S(1)}, bf16[1,80,1280]{2,1,0:T(8,128)(2,1)}, u32[]{:S(2)}) copy-start(bf16[1,80,1280]{2,1,0:T(8,128)(2,1)} %param.23) | copy-start | bytes 614404
  7.4 6.4 %copy-start.7 = (s32[1024]{0:T(1024)S(1)}, s32[1024]{0:T(1024)}, u32[]{:S(2)}) copy-start(s32[1024]{0:T(1024)} %param.29) | copy-start | bytes 12292
  7.4 6.5 %copy-start.11 = (s32[32,2]{0,1:T(2,128)S(1)}, s32[32,2]{0,1:T(2,128)}, u32[]{:S(2)}) copy-start(s32[32,2]{0,1:T(2,128)} %param.27) | copy-start | bytes 772
  7.4 6.6 %copy-start.10 = (s32[32]{0:T(128)S(1)}, s32[32]{0:T(128)}, u32[]{:S(2)}) copy-start(s32[32]{0:T(128)} %param.30) | copy-start | bytes 388
  7.4 129.1 %all-reduce.2.cloned.1.call-start = ((), (), s32[]{:S(2)}) async-start(), calls=%async_computation.1 | async-start | bytes 1310720 | tf_op jit(solution)/shard_map/psum | solution.py:120
  9.8 126.7 %copy-start.2 = (bf16[128,1280]{1,0:T(8,128)(2,1)S(1)}, bf16[128,1280]{1,0:T(8,128)(2,1)}, u32[]{:S(2)}) copy-start(bf16[128,1280]{1,0:T(8,128)(2,1)} %param.19) | copy-start | bytes 983044
  11.8 127.3 %copy-start.8 = (f32[1280]{0:T(1024)S(1)}, f32[1280]{0:T(1024)}, u32[]{:S(2)}) copy-start(f32[1280]{0:T(1024)} %param.25) | copy-start | bytes 15364
  11.8 127.3 %copy-start.9 = (f32[1280]{0:T(1024)S(1)}, f32[1280]{0:T(1024)}, u32[]{:S(2)}) copy-start(f32[1280]{0:T(1024)} %param.24) | copy-start | bytes 15364
  13.2 126.5 %all-gather.5.cloned.1.call-start = ((), (), s32[]{:S(2)}) async-start(), calls=%async_computation.2 | async-start | bytes 2703360 | tf_op jit(solution)/shard_map/all_gather | solution.py:125
  136.5 2.6 copy-start.3
  139.4 21.7 %copy-start.6 = (bf16[128,256]{1,0:T(8,128)(2,1)S(1)}, bf16[128,256]{1,0:T(8,128)(2,1)}, u32[]{:S(2)}) copy-start(bf16[128,256]{1,0:T(8,128)(2,1)} %param.32) | copy-start | bytes 196612
  139.6 60.3 %copy-start.12 = (f32[4096]{0:T(1024)S(1)}, f32[4096]{0:T(1024)}, u32[]{:S(2)}) copy-start(f32[4096]{0:T(1024)} %param.33) | copy-start | bytes 49156
  143.9 17.2 %all-to-all-start = ((bf16[32,2,128]{2,1,0:T(2,128)(2,1)}), bf16[32,2,128]{2,1,0:T(2,128)(2,1)S(1)}, u32[]{:S(2)}, u32[]{:S(2)}) async-start(bf16[32,2,128]{2,1,0:T(2,128)(2,1)} %reshape.793), calls=%async_computation | async-start | bytes 32768 | tf_op jit(solution)/shard_map/all_to_all | solution.py:144
  152.5 45.9 %all-gather.7.cloned.1.call-start = ((), (), s32[]{:S(2)}) async-start(), calls=%async_computation.3 | async-start | bytes 1114112 | tf_op jit(solution)/shard_map/all_gather | solution.py:166
  162.0 114.4 %all-gather.9.cloned.1.call-start = ((), (), s32[]{:S(2)}) async-start(), calls=%async_computation.4 | async-start | bytes 1081344 | tf_op jit(solution)/shard_map/all_gather | solution.py:198
  202.1 3.1 collective-permute-start
  205.8 149.8 %all-gather.11.cloned.1.call-start = ((), (), s32[]{:S(2)}) async-start(), calls=%async_computation.5 | async-start | bytes 1081344 | tf_op jit(solution)/shard_map/all_gather | solution.py:199
  207.8 3.2 copy-start.1
  212.2 23.3 %copy-start.4 = (bf16[256,4096]{1,0:T(8,128)(2,1)S(1)}, bf16[256,4096]{1,0:T(8,128)(2,1)}, u32[]{:S(2)}) copy-start(bf16[256,4096]{1,0:T(8,128)(2,1)} %copy.65) | copy-start | bytes 6291460
Sparse Core Ops, SparseCore 0:
  13.3 123.1 all-reduce.1
  162.1 36.2 all-gather.6
Sparse Core Ops, SparseCore 1:
  16.8 86.0 all-gather.4
  205.9 70.4 all-gather.8
  279.8 75.7 all-gather.10
where the time goes:
time: 380 us; the launch traced here: 376 us
  waiting for transfers between devices  282 us (74%)
  local copies, waits for them, and re-layouts  35 us (9%)
  matrix products  17.6 us (5%)
  between operations  15.5 us (4%)
  other arithmetic  14.2 us (4%)
  starting transfers between devices  11 us (3%)
    psum x1, waiting for transfers between devices, local(): branch_sum = lax.psum(branch_part, ('vis', 'tp'))  120 us
    all_gather x1, waiting for transfers between devices, local(): value_rows = lax.all_gather(values_here, 'ctx', axis=0, tiled=True)  77.6 us
    all_gather x1, waiting for transfers between devices, local(): key_rows = lax.all_gather(keys_here, 'ctx', axis=0, tiled=True)  38.7 us
    all_gather x1, waiting for transfers between devices, local(): full_rows = lax.all_gather(embeds, ('vis', 'tp'), axis=1, tiled=True)  36.3 us
    gather x2, local copies, waits for them, and re-layouts, local(): key_doc = jnp.take(doc_ids, key_pos)  23 us
    all_to_all x1, starting transfers between devices, local(): lax.all_to_all(outgoing.reshape(shards, send_each, slab_width), 'ctx', sp...  8.63 us
    all_to_all x1, waiting for transfers between devices, local(): lax.all_to_all(outgoing.reshape(shards, send_each, slab_width), 'ctx', sp...  8.54 us
  transfers between devices with their start and end apart: 7, of which 6 were waited for; matrix products, arithmetic and copies ran while one was open for 11% of the time, Pallas kernels for 0%

commit v1 on v0

v1 whole, which is shorter than its diff:
```python
import functools
import math

import jax
import jax.numpy as jnp
import numpy as np
from jax import lax
from jax.experimental import pallas as pl
from jax.experimental.pallas import tpu as pltpu
from jax.sharding import PartitionSpec as P

D = 4096
HD = 128
VD = 1280
VHD = 80
TOK = 128
NV, NX, NY, NT = 8, 4, 8, 2
NC = NX * NY

norm_eps = 1e-06
rope_base = 1000000.0
big_negative = -1e30
MESH = pl.DeviceIdType.MESH
F32 = jnp.float32
BF = jnp.bfloat16


def nn(a, b):
    return lax.dot_general(a, b, (((1,), (0,)), ((), ())), preferred_element_type=F32)


def nt(a, b):
    return lax.dot_general(a, b, (((1,), (1,)), ((), ())), preferred_element_type=F32)


def iota(shape, dim):
    return lax.broadcasted_iota(jnp.int32, shape, dim)


def hot(mask):
    return jnp.where(mask, 1.0, 0.0).astype(BF)


def layer_norm(values, scale_vec, shift_vec):
    centre = jnp.mean(values, axis=-1, keepdims=True)
    offset = values - centre
    spread = jnp.mean(offset * offset, axis=-1, keepdims=True)
    return offset * lax.rsqrt(spread + norm_eps) * scale_vec + shift_vec


def rotate(values, cosine, sine):
    return values * cosine + pltpu.roll(values, 64, 1) * sine


def angles_of(pos_column, freq_row):
    ang = pos_column * freq_row
    sign = jnp.where(iota(ang.shape, 1) < 64, -1.0, 1.0)
    return jnp.cos(ang), jnp.sin(ang) * sign


def fold(rows8):
    return jnp.concatenate([rows8[:, :640], rows8[:, 640:]], axis=0)


def unfold(rows16):
    return jnp.concatenate([rows16[:8], rows16[8:]], axis=1)


def kernel(
    patch, vgain, vbias, wqkv, vout, mgain, mbias, wblk, ipatch, wids, ipos, sorder, sorder_v, docs,
    text, ngain, wq_raw, wkv_in, freq, out,
    wq_land, wq, wkv, wbuf, tbuf, ntext, kvbuf, kibuf, blp, mixb, vo, pp, res,
    rs_src, rs_buf, ag, ysrc, ybuf, p4, nimg, qsrc, qbuf, kpos_s,
    lsem, x1s, x1r, vos, vor, ress, resr, ws, wr, ts, tr, rss, rsr, ags, agr, ys, yr,
    p4s, p4r, kvs, kvr, kis, kir, qs, qr, fs, fr,
):
    v, c, t = lax.axis_index("vis"), lax.axis_index("ctx"), lax.axis_index("tp")
    x, y = c // NY, lax.rem(c, NY)
    other = 1 - t

    def at_v(k):
        return (lax.rem(v + k, NV), c, t)

    def at_c(k):
        return (v, lax.rem(c + k, NC), t)

    def at_y(k):
        return (v, x * NY + lax.rem(y + k, NY), t)

    def at_x(k, tt):
        return (v, lax.rem(x + k, NX) * NY + y, tt)

    partner = (v, c, other)

    barrier = pltpu.get_barrier_semaphore()

    def greet(d):
        pl.semaphore_signal(barrier, inc=1, device_id=d, device_id_type=MESH)

    lax.fori_loop(1, NV, lambda k, z: (greet(at_v(k)), z)[1], 0)
    lax.fori_loop(1, NC, lambda k, z: (greet(at_c(k)), z)[1], 0)
    for k in range(1, NX):
        greet(at_x(k, other))
    greet(partner)
    greetings = (NV - 1) + (NC - 1) + (NX - 1) + 1

    loads = [
        pltpu.make_async_copy(wq_raw, wq_land, lsem.at[0]),
        pltpu.make_async_copy(wkv_in, wkv, lsem.at[1]),
        pltpu.make_async_copy(vout, vo.at[t], lsem.at[2]),
        pltpu.make_async_copy(text, tbuf.at[t, v], lsem.at[3]),
        pltpu.make_async_copy(wblk, wbuf.at[y], lsem.at[4]),
    ]
    for load in loads:
        load.start()

    def remote(src, dst, ssem, rsem, d):
        return pltpu.make_async_remote_copy(
            src_ref=src, dst_ref=dst, send_sem=ssem, recv_sem=rsem, device_id=d, device_id_type=MESH
        )

    normed = layer_norm(patch[...].astype(F32), vgain[...], vbias[...]).astype(BF)
    vq = nt(normed, wqkv[0:80, :]).astype(BF)
    vk = nt(normed, wqkv[80:160, :]).astype(BF)
    vv = nt(normed, wqkv[160:240, :]).astype(BF)
    wrow = wids[...]
    eye = iota((128, 128), 0) == iota((128, 128), 1)
    wcol = jnp.sum(jnp.where(eye, wrow, 0).astype(F32), axis=1, keepdims=True)
    scores = nt(vq, vk) / math.sqrt(VHD)
    scores = jnp.where(wcol == wrow.astype(F32), scores, big_negative)
    powers = jnp.exp(scores - jnp.max(scores, axis=-1, keepdims=True))
    totals = jnp.sum(powers, axis=-1, keepdims=True)
    blended = (nn(powers.astype(BF), vv) / totals).astype(BF)
    perm1 = hot(iota((128, 128), 1) == 4 * lax.rem(iota((128, 128), 0), 32) + iota((128, 128), 0) // 32)
    blp[...] = nn(perm1, blended).astype(BF).reshape(8, 16, VHD)
    pp[...] = nn(perm1, patch[...]).astype(BF).reshape(8, 16, VD)
    mixb[t, x] = blp[x * 2 + t]
    res[x] = pp[x * 2 + t]

    pl.semaphore_wait(barrier, greetings)

    x1 = []
    for k in range(NX):
        for dt in range(NT):
            if k + dt:
                tt = t if dt == 0 else other
                xx = lax.rem(x + k, NX)
                n = k * 2 + dt
                x1.append(remote(blp.at[xx * 2 + tt], mixb.at[t, x], x1s.at[n], x1r.at[n], at_x(k, tt)))
    for cp in x1:
        cp.start()
    for load in loads[2:]:
        load.wait()
    vo_cp = remote(vo.at[t], vo.at[t], vos, vor, partner)
    vo_cp.start()
    res_cp = []
    for k in range(1, NX):
        res_cp.append(remote(pp.at[lax.rem(x + k, NX) * 2 + t], res.at[x], ress.at[k], resr.at[k], at_x(k, t)))
        res_cp[-1].start()
    w_cp = [remote(wbuf.at[y], wbuf.at[y], ws.at[k], wr.at[k], at_y(k)) for k in range(1, NY)]
    for cp in w_cp:
        cp.start()
    t_cp = [remote(tbuf.at[t, v], tbuf.at[t, v], ts.at[k], tr.at[k], at_v(k)) for k in range(1, NV)]
    for cp in t_cp:
        cp.start()

    for cp in x1:
        cp.wait_recv()
    vo_cp.wait_recv()
    r64, c64 = iota((64, 64), 0), iota((64, 64), 1)
    perm2 = hot(c64 == (lax.rem(r64, 8) // 2) * 16 + (r64 // 8) * 2 + lax.rem(r64, 2))
    m0 = nn(perm2, mixb[0].reshape(64, VHD)).astype(BF)
    m1 = nn(perm2, mixb[1].reshape(64, VHD)).astype(BF)
    part = nn(m0, vo[0]) + nn(m1, vo[1])
    for k in range(NV):
        rs_src[k] = fold(part[8 * k : 8 * k + 8]).astype(BF)
    rs_cp = []
    for k in range(1, NV):
        cp = remote(rs_src.at[lax.rem(v + k, NV)], rs_buf.at[v], rss.at[k], rsr.at[k], at_v(k))
        cp.start()
        rs_cp.append(cp)
    rs_buf[v] = rs_src[v]

    for load in loads[:2]:
        load.wait()
    r256, c256 = iota((256, 256), 0), iota((256, 256), 1)
    perm_w = hot(c256 == 2 * lax.rem(r256, 128) + r256 // 128)

    def split_w(i, z):
        both = nn(perm_w, wq_land[pl.ds(pl.multiple_of(i * 256, 256), 256), :]).astype(BF)
        at = pl.ds(pl.multiple_of(i * 128, 128), 128)
        wq[at, 0:128] = both[:128]
        wq[at, 128:256] = both[128:]
        return z

    lax.fori_loop(0, 32, split_w, 0)

    for cp in res_cp:
        cp.wait_recv()
    pick = hot(iota((8, 64), 1) == (iota((8, 64), 0) // 2) * 16 + 2 * v + lax.rem(iota((8, 64), 0), 2))
    residual = nn(pick, res[...].reshape(64, VD))
    for cp in rs_cp:
        cp.wait_recv()
    summed = rs_buf[0].astype(F32)
    for k in range(1, NV):
        summed = summed + rs_buf[k].astype(F32)
    hidden = residual + unfold(summed)
    merged8 = layer_norm(hidden, mgain[...], mbias[...])
    ag[t, v] = fold(merged8).astype(BF)
    ag_cp = [remote(ag.at[t, v], ag.at[t, v], ags.at[k], agr.at[k], at_v(k)) for k in range(1, NV)]
    for cp in ag_cp:
        cp.start()

    for cp in t_cp:
        cp.wait_recv()
    t_fwd = remote(tbuf.at[t], tbuf.at[t], fs.at[0], fr.at[0], partner)
    t_fwd.start()

    s_own = sorder[c]
    slices = (s_own, 2 * NC - 1 - s_own)
    ip = ipos[...]
    lane1024 = iota((1, 1024), 1)
    ishard = lane1024 // 32
    patches = jnp.sum(ipatch[...].astype(F32), axis=0, keepdims=True)
    eye32 = iota((32, 32), 0) == iota((32, 32), 1)
    pcol = jnp.sum(jnp.where(eye32, patches, 0.0), axis=1, keepdims=True)
    live_all = (ishard == iota((32, 1024), 0)) & ((4 * lax.rem(lane1024, 32)).astype(F32) < pcol)
    live = jnp.sum(jnp.where(live_all, 1.0, 0.0), axis=0, keepdims=True)
    ipf = ip.astype(F32)
    rows_col = iota((128, 1), 0)
    own_pos = jnp.where(rows_col < 64, slices[0] * 64, slices[1] * 64) + lax.rem(rows_col, 64)
    own_pos_f = own_pos.astype(F32)
    hit = jnp.where((own_pos == ip) & (live > 0.5), 1.0, 0.0)
    is_image = jnp.sum(hit, axis=1, keepdims=True) > 0.5
    gather32 = hot(iota((1024, 32), 0) // 32 == iota((1024, 32), 1))
    place = nn(hit.astype(BF), gather32).astype(BF)
    own_doc = jnp.zeros((128, 128), F32)
    for j in range(32):
        blk = docs[:, 128 * j : 128 * j + 128].astype(F32)
        own_doc = own_doc + jnp.where(own_pos == iota((1, 128), 1) + 128 * j, blk, 0.0)
    own_doc = jnp.sum(own_doc, axis=1, keepdims=True)
    below = jnp.zeros((128, 128), F32)
    for j in range(32):
        blk = docs[:, 128 * j : 128 * j + 128].astype(F32)
        below = below + jnp.where(blk < own_doc, 1.0, 0.0)
    low = jnp.sum(below, axis=1, keepdims=True)
    own_slot = lane1024 == c * 32 + iota((32, 1024), 0)
    own_ipos = jnp.sum(jnp.where(own_slot, ipf, 0.0), axis=1, keepdims=True)
    so_col = jnp.sum(jnp.where(eye32, sorder_v[...].astype(F32), 0.0), axis=1, keepdims=True)
    sl = ip // 64
    pair = jnp.minimum(sl, 2 * NC - 1 - sl).astype(F32)
    goes = hot((pair == so_col) & (ishard == c))
    in_off = hot(lax.rem(ip, 64) == iota((64, 1024), 0))
    low_half = nt(hot((sl.astype(F32) == so_col) & (live > 0.5)), in_off)
    high_half = nt(hot((sl.astype(F32) == 2 * NC - 1 - so_col) & (live > 0.5)), in_off)
    gone = jnp.concatenate([low_half, high_half], axis=1)
    offset = iota((1, 128), 1)
    shard_pos = jnp.where(offset < 64, so_col * 64, (2 * NC - 1 - so_col) * 64) + lax.rem(offset, 64).astype(F32)
    shard_pos = jnp.where(gone > 0.5, 1e9, shard_pos)
    for e in range(NC):
        kpos_s[:, 128 * e : 128 * e + 128] = shard_pos[e : e + 1]
    ipos_live = jnp.where(live > 0.5, ipf, 1e9)
    gather32_t = hot(iota((32, 1024), 1) // 32 == iota((32, 1024), 0))
    place_t = nt(gather32_t, hit.astype(BF)) > 0.5
    low_row = jnp.sum(jnp.where(eye, low, 0.0), axis=0, keepdims=True)
    pos_row = jnp.sum(jnp.where(eye, own_pos_f, 0.0), axis=0, keepdims=True)
    low_i = jnp.sum(jnp.where(place_t, low_row, 0.0), axis=1, keepdims=True)
    pos_i = jnp.sum(jnp.where(place_t, pos_row, 0.0), axis=1, keepdims=True)
    fold32 = hot(lax.rem(iota((1024, 32), 0), 32) == iota((1024, 32), 1))
    select = nn(goes, fold32).astype(BF)
    cos_t, sin_t = angles_of(own_pos_f, freq[...])
    cos_i, sin_i = angles_of(own_ipos, freq[...])

    for cp in ag_cp:
        cp.wait_recv()
    ag_fwd = remote(ag.at[t], ag.at[t], fs.at[1], fr.at[1], partner)
    ag_fwd.start()
    for cp in w_cp:
        cp.wait_recv()
    ag_fwd.wait_recv()
    half_of, rest = r256 // 128, lax.rem(r256, 128)
    xs, j = rest // 32, lax.rem(rest, 32)
    perm3 = hot(c256 == (j // 16) * 128 + (lax.rem(j, 16) // 2) * 16 + half_of * 8 + xs * 2 + lax.rem(j, 2))
    mp = nn(perm3, ag[...].reshape(256, 640)).astype(BF)
    wg = wbuf[...].reshape(VD, 256)
    yv = nn(mp[:128], wg[:640]) + nn(mp[128:], wg[640:])
    ysrc[...] = yv.reshape(NX, 32, 256)
    y_cp = []
    for k in range(1, NX):
        cp = remote(ysrc.at[lax.rem(x + k, NX)], ybuf.at[x], ys.at[k], yr.at[k], at_x(k, t))
        cp.start()
        y_cp.append(cp)
    ybuf[x] = ysrc[x]

    t_fwd.wait_recv()

    def normalise(buf, dst, rows):
        def squares(i, total):
            blk = buf[lax.rem(i, 2), i // 2].astype(F32)
            return total + jnp.sum(blk * blk, axis=1, keepdims=True)

        total = lax.fori_loop(0, 16, squares, jnp.zeros((rows, 1), F32))
        scale = lax.rsqrt(total * (1.0 / D) + norm_eps)
        for i in range(16):
            cols = slice(256 * i, 256 * i + 256)
            dst[:, cols] = (buf[i % 2, i // 2].astype(F32) * scale * ngain[:, cols]).astype(BF)

    normalise(tbuf, ntext, TOK)
    kv_t = nn(ntext[...], wkv[...])
    kvbuf[t, c] = jnp.where(t == 0, rotate(kv_t, cos_t, sin_t), kv_t).astype(BF)

    def kv_copy(k):
        return remote(kvbuf.at[t, c], kvbuf.at[t, c], kvs.at[k], kvr.at[k], at_c(k))

    lax.fori_loop(1, NC, lambda k, z: (kv_copy(k).start(), z)[1], 0)

    for cp in y_cp:
        cp.wait_recv()
    emb = ybuf[0]
    for k in range(1, NX):
        emb = emb + ybuf[k]
    p4[t, v] = emb.astype(BF)
    p4_cp = [remote(p4.at[t, v], p4.at[t, v], p4s.at[k], p4r.at[k], at_v(k)) for k in range(1, NV)]
    for cp in p4_cp:
        cp.start()
    q_t = nn(ntext[...], wq[...])
    q_t = [rotate(q_t[:, :128], cos_t, sin_t).astype(BF), rotate(q_t[:, 128:], cos_t, sin_t).astype(BF)]

    for cp in p4_cp:
        cp.wait_recv()
    p4_fwd = remote(p4.at[t], p4.at[t], fs.at[2], fr.at[2], partner)
    p4_fwd.start()
    p4_fwd.wait_recv()
    normalise(p4, nimg, 32)
    q_i = nn(nimg[...], wq[...])
    q_i = jnp.concatenate(
        [rotate(q_i[:, :128], cos_i, sin_i), rotate(q_i[:, 128:], cos_i, sin_i)], axis=1
    ).astype(BF)
    q_go = nn(select, q_i)
    for e in range(NC):
        qsrc[e] = q_go[e : e + 1]
    qbuf[c] = qsrc[c]

    def q_copy(k):
        return remote(qsrc.at[lax.rem(c + k, NC)], qbuf.at[c], qs.at[k], qr.at[k], at_c(k))

    kv_i = nn(nimg[...], wkv[...])
    kibuf[t, c] = jnp.where(t == 0, rotate(kv_i, cos_i, sin_i), kv_i).astype(BF)

    def ki_copy(k):
        return remote(kibuf.at[t, c], kibuf.at[t, c], kis.at[k], kir.at[k], at_c(k))

    lax.fori_loop(1, NC, lambda k, z: (ki_copy(k).start(), z)[1], 0)
    lax.fori_loop(1, NC, lambda k, z: (q_copy(k).start(), z)[1], 0)

    lax.fori_loop(1, NC, lambda k, z: (kv_copy(k).wait_recv(), z)[1], 0)
    kv_fwd = remote(kvbuf.at[t], kvbuf.at[t], fs.at[3], fr.at[3], partner)
    kv_fwd.start()
    lax.fori_loop(1, NC, lambda k, z: (ki_copy(k).wait_recv(), z)[1], 0)
    ki_fwd = remote(kibuf.at[t], kibuf.at[t], fs.at[4], fr.at[4], partner)
    ki_fwd.start()
    lax.fori_loop(1, NC, lambda k, z: (q_copy(k).wait_recv(), z)[1], 0)
    q_in = jnp.concatenate([qbuf[e] for e in range(NC)], axis=0).astype(BF)
    kv_fwd.wait_recv()
    pos2, low2 = jnp.concatenate([own_pos_f] * 2, axis=0), jnp.concatenate([low] * 2, axis=0)
    pos2_i, low2_i = jnp.concatenate([pos_i] * 2, axis=0), jnp.concatenate([low_i] * 2, axis=0)
    qq = jnp.concatenate([q_t[0], q_t[1], q_in[:, :128], q_in[:, 128:]], axis=0)
    qq_pos = jnp.concatenate([pos2, pos2_i], axis=0)
    qq_low = jnp.concatenate([low2, low2_i], axis=0)
    scale = 1.0 / math.sqrt(HD)

    def attend(state, keys, values, kpos):
        best, total, acc = state
        s = nt(qq, keys) * scale
        s = jnp.where((kpos >= qq_low) & (kpos <= qq_pos), s, big_negative)
        new = jnp.maximum(best, jnp.max(s, axis=1, keepdims=True))
        factor = jnp.exp(best - new)
        p = jnp.exp(s - new)
        total = total * factor + jnp.sum(p, axis=1, keepdims=True)
        return new, total, acc * factor + nn(p.astype(BF), values)

    rows = qq.shape[0]
    state = (jnp.full((rows, 1), big_negative, F32), jnp.zeros((rows, 1), F32), jnp.zeros((rows, HD), F32))
    for b in range(4):
        keys = kvbuf[0, 8 * b : 8 * b + 8].reshape(1024, HD)
        values = kvbuf[1, 8 * b : 8 * b + 8].reshape(1024, HD)
        state = attend(state, keys, values, kpos_s[:, 1024 * b : 1024 * b + 1024])
    ki_fwd.wait_recv()
    state = attend(state, kibuf[0].reshape(1024, HD), kibuf[1].reshape(1024, HD), ipos_live)
    result = (state[2] / state[1]).astype(BF)
    for g in range(2):
        placed = nn(place, result[256 + 32 * g : 288 + 32 * g])
        mixed = jnp.where(is_image, placed, result[128 * g : 128 * g + 128].astype(F32))
        out[:, 128 * g : 128 * g + 128] = mixed.astype(BF)

    for cp in x1 + [vo_cp] + res_cp + w_cp + t_cp + rs_cp + ag_cp + y_cp + p4_cp:
        cp.wait_send()
    for cp in (t_fwd, ag_fwd, p4_fwd, kv_fwd, ki_fwd):
        cp.wait_send()
    lax.fori_loop(1, NC, lambda k, z: (kv_copy(k).wait_send(), ki_copy(k).wait_send(), q_copy(k).wait_send(), z)[3], 0)


def local(
    patch_rows, vit_gain, vit_bias, vit_qkv, vit_out, merge_gain, merge_bias, merge_weight,
    image_patches, window_ids, image_pos, slice_order, doc_ids, text_rows, norm_gain, w_query, w_keyval,
):
    exponent = np.arange(64, dtype=np.float64) * (-2.0 / HD)
    freq = np.power(np.float64(rope_base), exponent).astype(np.float32)
    freq = jnp.asarray(np.concatenate([freq, freq])[None, :])
    vm = pl.BlockSpec(memory_space=pltpu.VMEM)
    hbm = pl.BlockSpec(memory_space=pl.ANY)
    sm = pl.BlockSpec(memory_space=pltpu.SMEM)
    dma = pltpu.SemaphoreType.DMA
    args = [
        (patch_rows, vm),
        (vit_gain.reshape(1, VD), vm),
        (vit_bias.reshape(1, VD), vm),
        (jnp.transpose(vit_qkv, (1, 2, 3, 0)).reshape(3 * VHD, VD), vm),
        (vit_out.reshape(VHD, VD), hbm),
        (merge_gain.reshape(1, VD), vm),
        (merge_bias.reshape(1, VD), vm),
        (merge_weight, hbm),
        (jnp.transpose(image_patches), vm),
        (window_ids.reshape(1, 128), vm),
        (image_pos.reshape(1, 1024), vm),
        (slice_order, sm),
        (slice_order.reshape(1, NC), vm),
        (doc_ids.reshape(1, 4096), vm),
        (text_rows, hbm),
        (norm_gain.reshape(1, D), vm),
        (w_query.reshape(2 * D, HD), hbm),
        (w_keyval.reshape(D, HD), hbm),
        (freq, vm),
    ]
    scratch = [
        pltpu.VMEM((2 * D, HD), BF),
        pltpu.VMEM((D, 2 * HD), BF),
        pltpu.VMEM((D, HD), BF),
        pltpu.VMEM((NY, 160, 256), BF),
        pltpu.VMEM((NT, NV, TOK, 256), BF),
        pltpu.VMEM((TOK, D), BF),
        pltpu.VMEM((NT, NC, TOK, HD), BF),
        pltpu.VMEM((NT, NC, 32, HD), BF),
        pltpu.VMEM((8, 16, VHD), BF),
        pltpu.VMEM((NT, NX, 16, VHD), BF),
        pltpu.VMEM((NT, VHD, VD), BF),
        pltpu.VMEM((8, 16, VD), BF),
        pltpu.VMEM((NX, 16, VD), BF),
        pltpu.VMEM((NV, 16, 640), BF),
        pltpu.VMEM((NV, 16, 640), BF),
        pltpu.VMEM((NT, NV, 16, 640), BF),
        pltpu.VMEM((NX, 32, 256), F32),
        pltpu.VMEM((NX, 32, 256), F32),
        pltpu.VMEM((NT, NV, 32, 256), BF),
        pltpu.VMEM((32, D), BF),
        pltpu.VMEM((NC, 1, 256), F32),
        pltpu.VMEM((NC, 1, 256), F32),
        pltpu.VMEM((1, 4096), F32),
        dma((5,)),
        dma((8,)), dma((8,)),
        dma, dma,
        dma((NX,)), dma((NX,)),
        dma((NY,)), dma((NY,)),
        dma((NV,)), dma((NV,)),
        dma((NV,)), dma((NV,)),
        dma((NV,)), dma((NV,)),
        dma((NX,)), dma((NX,)),
        dma((NV,)), dma((NV,)),
        dma((NC,)), dma((NC,)),
        dma((NC,)), dma((NC,)),
        dma((NC,)), dma((NC,)),
        dma((5,)), dma((5,)),
    ]
    result = pl.pallas_call(
        kernel,
        name="fused",
        out_shape=jax.ShapeDtypeStruct((TOK, 256), BF),
        in_specs=[spec for _, spec in args],
        out_specs=vm,
        scratch_shapes=scratch,
        compiler_params=pltpu.CompilerParams(
            collective_id=0, has_side_effects=True, vmem_limit_bytes=48 << 20
        ),
    )(*[value for value, _ in args])
    return result.reshape(TOK, 1, 256)


def solution(mesh):
    placed = (
        P("ctx", None),
        P(),
        P(),
        P(None, None, ("vis", "tp"), None),
        P(("vis", "tp"), None, None),
        P(),
        P(),
        P("ctx", ("vis", "tp")),
        P(),
        P("ctx"),
        P(),
        P(),
        P(),
        P("ctx", ("vis", "tp")),
        P(),
        P(None, "vis", "tp", None),
        P("tp", None, "vis", None),
    )
    return jax.shard_map(
        local, mesh=mesh, in_specs=placed, out_specs=P("ctx", "vis", "tp"), check_vma=False
    )
```

time: 380 us -> 101 us (0.27)
  waiting for transfers between devices: 282 us -> 0 us
  Pallas kernels: 0 us -> 84.2 us
  local copies, waits for them, and re-layouts: 35 us -> 15.7 us
  matrix products: 17.6 us -> 0 us
  between operations: 15.5 us -> 0.03 us
  other arithmetic: 14.2 us -> 0 us
  starting transfers between devices: 11 us -> 0 us
    all_gather x4 -> x0, waiting for transfers between devices: 153 us -> none  [the longest x1 77.6 us: local(): value_rows = lax.all_gather(values_here, 'ctx', axis=0, tiled=True)]
    psum x1 -> x0, waiting for transfers between devices: 120 us -> none  [local(): branch_sum = lax.psum(branch_part, ('vis', 'tp'))]
    pallas_call x0 -> x1, Pallas kernels: none -> 84.2 us  [local(): pl.pallas_call(kernel, name='fused', out_shape=jax.ShapeDtypeStruct((TOK,...]
    gather x3 -> x0, local copies, waits for them, and re-layouts: 24.2 us -> none  [the longest x2 23 us: local(): key_doc = jnp.take(doc_ids, key_pos)]
    dot_general x16 -> x0, matrix products: 17.6 us -> none  [the longest x4 5.5 us: key_block(): jnp.einsum('kgqn,nkd->kgqd', powers_now.astype(jnp.bfloat16), values_blk,...]
    all_to_all x1 -> x0, starting transfers between devices: 8.63 us -> none  [local(): lax.all_to_all(outgoing.reshape(shards, send_each, slab_width), 'ctx', sp...]
    reduce_sum x15 -> x0, other arithmetic: 8.61 us -> none  [the longest x2 2.51 us: layer_norm(): spread = jnp.mean(offset * offset, axis=-1, keepdims=True)]
    all_to_all x1 -> x0, waiting for transfers between devices: 8.54 us -> none  [local(): lax.all_to_all(outgoing.reshape(shards, send_each, slab_width), 'ctx', sp...]
  transfers between devices with their start and end apart: 7 -> 0, of which waited for: 6 -> 0; matrix products, arithmetic and copies ran while one was open for 11% -> 0% of each run, Pallas kernels for 0% -> 0%
where the time goes in v1:
time: 101 us; the launch traced here: 100 us
  Pallas kernels  84.2 us (83%)
  local copies, waits for them, and re-layouts  15.7 us (16%)
    pallas_call x1, Pallas kernels, local(): pl.pallas_call(kernel, name='fused', out_shape=jax.ShapeDtypeStruct((TOK,...  84.2 us
    unnamed x29, local copies, waits for them, and re-layouts  12.9 us

profile of v1, /device:TPU:1, one launch (start us, length us, event | category | flops | bytes accessed | tf_op | source)
XLA Modules:
  0.0 100.0 jit_solution(5949913624582555581)
XLA Ops:
  0.0 0.7 reshape.42.vgain
  0.7 0.7 reshape.43.vbias
  1.4 0.7 reshape.46.mgain
  2.1 0.7 reshape.47.mbias
  2.8 0.0 copy-start
  2.8 1.6 %copy-done = bf16[4096,1,2,128]{3,2,1,0:T(2,128)(2,1)S(1)} copy-done((bf16[4096,1,2,128]{3,2,1,0:T(2,128)(2,1)S(1)}, bf16[4096,1,2,128]{3,2,1,0:T(2,128)(2,1)}, u32[]{:S(2)}) %copy-start) | copy-done | bytes 2097176
  4.4 0.0 copy-start.1
  4.4 1.2 %copy-done.1 = bf16[1,4096,1,128]{3,1,2,0:T(8,128)(2,1)S(1)} copy-done((bf16[1,4096,1,128]{3,1,2,0:T(8,128)(2,1)S(1)}, bf16[1,4096,1,128]{3,1,2,0:T(8,128)(2,1)}, u32[]{:S(2)}) %copy-start.1) | copy-done | bytes 1048600
  5.6 0.0 copy-start.2
  5.6 1.1 %copy-done.2 = bf16[1280,3,1,80]{0,3,2,1:T(8,128)(2,1)S(1)} copy-done((bf16[1280,3,1,80]{0,3,2,1:T(8,128)(2,1)S(1)}, bf16[1280,3,1,80]{0,3,2,1:T(8,128)(2,1)}, u32[]{:S(2)}) %copy-start.2) | copy-done | bytes 614424
  6.7 0.0 copy-start.3
  6.7 1.0 copy-done.3
  7.7 0.0 copy-start.4
  7.7 0.9 copy-done.4
  8.6 0.0 copy-start.5
  8.6 0.9 copy-done.5
  9.5 0.0 copy-start.6
  9.5 0.8 copy-done.6
  10.3 0.0 copy-start.7
  10.3 0.7 copy-done.7
  11.0 0.0 copy-start.8
  11.0 0.7 copy-done.8
  11.8 0.0 copy-start.9
  11.8 0.7 copy-done.9
  12.4 0.0 copy-start.10
  12.5 0.7 copy-done.10
  13.1 0.0 copy-start.11
  13.1 0.7 copy-done.11
  13.8 0.0 copy-start.12
  13.8 0.7 copy-done.12
  14.4 0.0 copy-start.13
  14.4 0.7 copy-done.13
  15.1 84.2 %fused.1 = bf16[128,256]{1,0:T(8,128)(2,1)S(1)} custom-call(bf16[128,1280]{1,0:T(8,128)(2,1)S(1)} %copy-done.3, f32[1,1280]{1,0:T(1,128)S(1)} %reshape.42.vgain, f32[1,1280]{1,0:T(1,128)S(1)} %reshape.43.vbias, bf16[240,1280]{1,0:T(8,128)(2,1)S(1)} %bitcast.15, bf16[80,1280]{1,0:T(8,128)(2,1)S(1)} %bitcast.17, f32[1,1280]{1,0:T(1,128)S(1)} %reshape.46.mgain, ...), custom_call_target="tpu_custom_call" | custom-call | tf_op jit(solution)/shard_map/fused/pallas_call | solution.py:474
  99.3 0.6 copy.20
Async XLA Ops:
  2.8 1.6 %copy-start = (bf16[4096,1,2,128]{3,2,1,0:T(2,128)(2,1)S(1)}, bf16[4096,1,2,128]{3,2,1,0:T(2,128)(2,1)}, u32[]{:S(2)}) copy-start(bf16[4096,1,2,128]{3,2,1,0:T(2,128)(2,1)} %param.33) | copy-start | bytes 6291460
  4.4 1.2 %copy-start.1 = (bf16[1,4096,1,128]{3,1,2,0:T(8,128)(2,1)S(1)}, bf16[1,4096,1,128]{3,1,2,0:T(8,128)(2,1)}, u32[]{:S(2)}) copy-start(bf16[1,4096,1,128]{3,1,2,0:T(8,128)(2,1)} %param.34) | copy-start | bytes 3145732
  5.6 1.1 %copy-start.2 = (bf16[1280,3,1,80]{0,3,2,1:T(8,128)(2,1)S(1)}, bf16[1280,3,1,80]{0,3,2,1:T(8,128)(2,1)}, u32[]{:S(2)}) copy-start(bf16[1280,3,1,80]{0,3,2,1:T(8,128)(2,1)} %param.21) | copy-start | bytes 1843204
  6.7 1.0 copy-start.3
  7.7 0.9 copy-start.4
  8.6 0.9 copy-start.5
  9.5 0.8 copy-start.6
  10.3 0.7 copy-start.7
  11.0 0.7 copy-start.8
  11.8 0.7 copy-start.9
  12.4 0.7 copy-start.10
  13.1 0.7 copy-start.11
  13.8 0.7 copy-start.12
  14.4 0.7 copy-start.13

commit v2 on v1

--- a/solution.py
+++ b/solution.py
@@ -67,8 +67,9 @@
 
 
 def kernel(
-    patch, vgain, vbias, wqkv, vout, mgain, mbias, wblk, ipatch, wids, ipos, sorder, sorder_v, docs,
-    text, ngain, wq_raw, wkv_in, freq, out,
+    patch_h, vgain_h, vbias_h, wqkv_h, vout, mgain_h, mbias_h, wblk, ipatch_h, wids_h, ipos_h, sorder_h, docs_h,
+    text, ngain_h, wq_raw, wkv_in, freq_h, out,
+    patch, vgain, vbias, wqkv, mgain, mbias, ipatch, wids, ipos, sorder, sorder_v, docs, ngain, freq,
     wq_land, wq, wkv, wbuf, tbuf, ntext, kvbuf, kibuf, blp, mixb, vo, pp, res,
     rs_src, rs_buf, ag, ysrc, ybuf, p4, nimg, qsrc, qbuf, kpos_s,
     lsem, x1s, x1r, vos, vor, ress, resr, ws, wr, ts, tr, rss, rsr, ags, agr, ys, yr,
@@ -92,6 +93,16 @@
 
     partner = (v, c, other)
 
+    pairs = [
+        (patch_h, patch), (vgain_h, vgain), (vbias_h, vbias), (wqkv_h, wqkv), (wids_h, wids),
+        (vout, vo.at[t]), (text, tbuf.at[t, v]), (wblk, wbuf.at[y]),
+        (wq_raw, wq_land), (mgain_h, mgain), (mbias_h, mbias), (ipatch_h, ipatch), (ipos_h, ipos),
+        (sorder_h, sorder_v), (sorder_h, sorder), (docs_h, docs), (ngain_h, ngain), (freq_h, freq), (wkv_in, wkv),
+    ]
+    loads = [pltpu.make_async_copy(a, b, lsem.at[n]) for n, (a, b) in enumerate(pairs)]
+    for load in loads:
+        load.start()
+
     barrier = pltpu.get_barrier_semaphore()
 
     def greet(d):
@@ -104,22 +115,15 @@
     greet(partner)
     greetings = (NV - 1) + (NC - 1) + (NX - 1) + 1
 
-    loads = [
-        pltpu.make_async_copy(wq_raw, wq_land, lsem.at[0]),
-        pltpu.make_async_copy(wkv_in, wkv, lsem.at[1]),
-        pltpu.make_async_copy(vout, vo.at[t], lsem.at[2]),
-        pltpu.make_async_copy(text, tbuf.at[t, v], lsem.at[3]),
-        pltpu.make_async_copy(wblk, wbuf.at[y], lsem.at[4]),
-    ]
-    for load in loads:
-        load.start()
 
     def remote(src, dst, ssem, rsem, d):
         return pltpu.make_async_remote_copy(
             src_ref=src, dst_ref=dst, send_sem=ssem, recv_sem=rsem, device_id=d, device_id_type=MESH
         )
 
-    normed = layer_norm(patch[...].astype(F32), vgain[...], vbias[...]).astype(BF)
+    for load in loads[:5]:
+        load.wait()
+    normed = layer_norm(patch[...].astype(F32), vgain[...].reshape(1, VD), vbias[...].reshape(1, VD)).astype(BF)
     vq = nt(normed, wqkv[0:80, :]).astype(BF)
     vk = nt(normed, wqkv[80:160, :]).astype(BF)
     vv = nt(normed, wqkv[160:240, :]).astype(BF)
@@ -149,7 +153,7 @@
                 x1.append(remote(blp.at[xx * 2 + tt], mixb.at[t, x], x1s.at[n], x1r.at[n], at_x(k, tt)))
     for cp in x1:
         cp.start()
-    for load in loads[2:]:
+    for load in loads[5:8]:
         load.wait()
     vo_cp = remote(vo.at[t], vo.at[t], vos, vor, partner)
     vo_cp.start()
@@ -157,13 +161,14 @@
     for k in range(1, NX):
         res_cp.append(remote(pp.at[lax.rem(x + k, NX) * 2 + t], res.at[x], ress.at[k], resr.at[k], at_x(k, t)))
         res_cp[-1].start()
+    t_cp = {
+        k: remote(tbuf.at[t, v], tbuf.at[t, v], ts.at[k], tr.at[k], at_v(k)) for k in range(1, NV)
+    }
+    for k in (1, 7, 2, 6):
+        t_cp[k].start()
     w_cp = [remote(wbuf.at[y], wbuf.at[y], ws.at[k], wr.at[k], at_y(k)) for k in range(1, NY)]
     for cp in w_cp:
         cp.start()
-    t_cp = [remote(tbuf.at[t, v], tbuf.at[t, v], ts.at[k], tr.at[k], at_v(k)) for k in range(1, NV)]
-    for cp in t_cp:
-        cp.start()
-
     for cp in x1:
         cp.wait_recv()
     vo_cp.wait_recv()
@@ -180,8 +185,10 @@
         cp.start()
         rs_cp.append(cp)
     rs_buf[v] = rs_src[v]
-
-    for load in loads[:2]:
+    for k in (3, 5, 4):
+        t_cp[k].start()
+
+    for load in loads[8:]:
         load.wait()
     r256, c256 = iota((256, 256), 0), iota((256, 256), 1)
     perm_w = hot(c256 == 2 * lax.rem(r256, 128) + r256 // 128)
@@ -195,28 +202,7 @@
 
     lax.fori_loop(0, 32, split_w, 0)
 
-    for cp in res_cp:
-        cp.wait_recv()
-    pick = hot(iota((8, 64), 1) == (iota((8, 64), 0) // 2) * 16 + 2 * v + lax.rem(iota((8, 64), 0), 2))
-    residual = nn(pick, res[...].reshape(64, VD))
-    for cp in rs_cp:
-        cp.wait_recv()
-    summed = rs_buf[0].astype(F32)
-    for k in range(1, NV):
-        summed = summed + rs_buf[k].astype(F32)
-    hidden = residual + unfold(summed)
-    merged8 = layer_norm(hidden, mgain[...], mbias[...])
-    ag[t, v] = fold(merged8).astype(BF)
-    ag_cp = [remote(ag.at[t, v], ag.at[t, v], ags.at[k], agr.at[k], at_v(k)) for k in range(1, NV)]
-    for cp in ag_cp:
-        cp.start()
-
-    for cp in t_cp:
-        cp.wait_recv()
-    t_fwd = remote(tbuf.at[t], tbuf.at[t], fs.at[0], fr.at[0], partner)
-    t_fwd.start()
-
-    s_own = sorder[c]
+    s_own = sorder[0, c]
     slices = (s_own, 2 * NC - 1 - s_own)
     ip = ipos[...]
     lane1024 = iota((1, 1024), 1)
@@ -258,7 +244,7 @@
     shard_pos = jnp.where(offset < 64, so_col * 64, (2 * NC - 1 - so_col) * 64) + lax.rem(offset, 64).astype(F32)
     shard_pos = jnp.where(gone > 0.5, 1e9, shard_pos)
     for e in range(NC):
-        kpos_s[:, 128 * e : 128 * e + 128] = shard_pos[e : e + 1]
+        kpos_s[e // 8, :, 128 * (e % 8) : 128 * (e % 8) + 128] = shard_pos[e : e + 1]
     ipos_live = jnp.where(live > 0.5, ipf, 1e9)
     gather32_t = hot(iota((32, 1024), 1) // 32 == iota((32, 1024), 0))
     place_t = nt(gather32_t, hit.astype(BF)) > 0.5
@@ -270,6 +256,48 @@
     select = nn(goes, fold32).astype(BF)
     cos_t, sin_t = angles_of(own_pos_f, freq[...])
     cos_i, sin_i = angles_of(own_ipos, freq[...])
+
+    for cp in res_cp:
+        cp.wait_recv()
+    pick = hot(iota((8, 64), 1) == (iota((8, 64), 0) // 2) * 16 + 2 * v + lax.rem(iota((8, 64), 0), 2))
+    residual = nn(pick, res[...].reshape(64, VD))
+    for cp in rs_cp:
+        cp.wait_recv()
+    summed = rs_buf[0].astype(F32)
+    for k in range(1, NV):
+        summed = summed + rs_buf[k].astype(F32)
+    hidden = residual + unfold(summed)
+    merged8 = layer_norm(hidden, mgain[...].reshape(1, VD), mbias[...].reshape(1, VD))
+    ag[t, v] = fold(merged8).astype(BF)
+    ag_cp = [remote(ag.at[t, v], ag.at[t, v], ags.at[k], agr.at[k], at_v(k)) for k in range(1, NV)]
+    for cp in ag_cp:
+        cp.start()
+
+    for k in range(1, NV):
+        t_cp[k].wait_recv()
+    t_fwd = remote(tbuf.at[t], tbuf.at[t], fs.at[0], fr.at[0], partner)
+    t_fwd.start()
+    t_fwd.wait_recv()
+
+    def normalise(buf, dst, rows):
+        def squares(i, total):
+            blk = buf[lax.rem(i, 2), i // 2].astype(F32)
+            return total + jnp.sum(blk * blk, axis=1, keepdims=True)
+
+        total = lax.fori_loop(0, 16, squares, jnp.zeros((rows, 1), F32))
+        scale = lax.rsqrt(total * (1.0 / D) + norm_eps)
+        for i in range(16):
+            cols = slice(256 * i, 256 * i + 256)
+            dst[:, cols] = (buf[i % 2, i // 2].astype(F32) * scale * ngain[:, cols]).astype(BF)
+
+    normalise(tbuf, ntext, TOK)
+    kv_t = nn(ntext[...], wkv[...])
+    kvbuf[t, c] = jnp.where(t == 0, rotate(kv_t, cos_t, sin_t), kv_t).astype(BF)
+
+    def kv_copy(k):
+        return remote(kvbuf.at[t, c], kvbuf.at[t, c], kvs.at[k], kvr.at[k], at_c(k))
+
+    lax.fori_loop(1, NC, lambda k, z: (kv_copy(k).start(), z)[1], 0)
 
     for cp in ag_cp:
         cp.wait_recv()
@@ -292,28 +320,6 @@
         y_cp.append(cp)
     ybuf[x] = ysrc[x]
 
-    t_fwd.wait_recv()
-
-    def normalise(buf, dst, rows):
-        def squares(i, total):
-            blk = buf[lax.rem(i, 2), i // 2].astype(F32)
-            return total + jnp.sum(blk * blk, axis=1, keepdims=True)
-
-        total = lax.fori_loop(0, 16, squares, jnp.zeros((rows, 1), F32))
-        scale = lax.rsqrt(total * (1.0 / D) + norm_eps)
-        for i in range(16):
-            cols = slice(256 * i, 256 * i + 256)
-            dst[:, cols] = (buf[i % 2, i // 2].astype(F32) * scale * ngain[:, cols]).astype(BF)
-
-    normalise(tbuf, ntext, TOK)
-    kv_t = nn(ntext[...], wkv[...])
-    kvbuf[t, c] = jnp.where(t == 0, rotate(kv_t, cos_t, sin_t), kv_t).astype(BF)
-
-    def kv_copy(k):
-        return remote(kvbuf.at[t, c], kvbuf.at[t, c], kvs.at[k], kvr.at[k], at_c(k))
-
-    lax.fori_loop(1, NC, lambda k, z: (kv_copy(k).start(), z)[1], 0)
-
     for cp in y_cp:
         cp.wait_recv()
     emb = ybuf[0]
@@ -356,44 +362,60 @@
     lax.fori_loop(1, NC, lambda k, z: (kv_copy(k).wait_recv(), z)[1], 0)
     kv_fwd = remote(kvbuf.at[t], kvbuf.at[t], fs.at[3], fr.at[3], partner)
     kv_fwd.start()
+    kv_fwd.wait_recv()
+    scale = 1.0 / math.sqrt(HD)
+
+    def attend(state, queries, qpos, qlow, keys, values, kpos):
+        best, total, acc = state
+        sc = nt(queries, keys) * scale
+        sc = jnp.where((kpos >= qlow) & (kpos <= qpos), sc, big_negative)
+        new = jnp.maximum(best, jnp.max(sc, axis=1, keepdims=True))
+        factor = jnp.exp(best - new)
+        p = jnp.exp(sc - new)
+        total = total * factor + jnp.sum(p, axis=1, keepdims=True)
+        return new, total, acc * factor + nn(p.astype(BF), values)
+
+    def over_text(queries, qpos, qlow):
+        rows = queries.shape[0]
+        state = (jnp.full((rows, 1), big_negative, F32), jnp.zeros((rows, 1), F32), jnp.zeros((rows, HD), F32))
+
+        def block(b, state):
+            at = pl.ds(b * 8, 8)
+            keys = kvbuf[0, at].reshape(1024, HD)
+            values = kvbuf[1, at].reshape(1024, HD)
+            return attend(state, queries, qpos, qlow, keys, values, kpos_s[b])
+
+        return lax.fori_loop(0, 4, block, state)
+
+    queries_t = jnp.concatenate(q_t, axis=0)
+    pos2, low2 = jnp.concatenate([own_pos_f] * 2, axis=0), jnp.concatenate([low] * 2, axis=0)
+    state_t = over_text(queries_t, pos2, low2)
+
     lax.fori_loop(1, NC, lambda k, z: (ki_copy(k).wait_recv(), z)[1], 0)
     ki_fwd = remote(kibuf.at[t], kibuf.at[t], fs.at[4], fr.at[4], partner)
     ki_fwd.start()
     lax.fori_loop(1, NC, lambda k, z: (q_copy(k).wait_recv(), z)[1], 0)
     q_in = jnp.concatenate([qbuf[e] for e in range(NC)], axis=0).astype(BF)
-    kv_fwd.wait_recv()
-    pos2, low2 = jnp.concatenate([own_pos_f] * 2, axis=0), jnp.concatenate([low] * 2, axis=0)
+    queries_i = jnp.concatenate([q_in[:, :128], q_in[:, 128:]], axis=0)
     pos2_i, low2_i = jnp.concatenate([pos_i] * 2, axis=0), jnp.concatenate([low_i] * 2, axis=0)
-    qq = jnp.concatenate([q_t[0], q_t[1], q_in[:, :128], q_in[:, 128:]], axis=0)
-    qq_pos = jnp.concatenate([pos2, pos2_i], axis=0)
-    qq_low = jnp.concatenate([low2, low2_i], axis=0)
-    scale = 1.0 / math.sqrt(HD)
-
-    def attend(state, keys, values, kpos):
-        best, total, acc = state
-        s = nt(qq, keys) * scale
-        s = jnp.where((kpos >= qq_low) & (kpos <= qq_pos), s, big_negative)
-        new = jnp.maximum(best, jnp.max(s, axis=1, keepdims=True))
-        factor = jnp.exp(best - new)
-        p = jnp.exp(s - new)
-        total = total * factor + jnp.sum(p, axis=1, keepdims=True)
-        return new, total, acc * factor + nn(p.astype(BF), values)
-
-    rows = qq.shape[0]
-    state = (jnp.full((rows, 1), big_negative, F32), jnp.zeros((rows, 1), F32), jnp.zeros((rows, HD), F32))
-    for b in range(4):
-        keys = kvbuf[0, 8 * b : 8 * b + 8].reshape(1024, HD)
-        values = kvbuf[1, 8 * b : 8 * b + 8].reshape(1024, HD)
-        state = attend(state, keys, values, kpos_s[:, 1024 * b : 1024 * b + 1024])
+    state_i = over_text(queries_i, pos2_i, low2_i)
     ki_fwd.wait_recv()
-    state = attend(state, kibuf[0].reshape(1024, HD), kibuf[1].reshape(1024, HD), ipos_live)
+    state = attend(
+        [jnp.concatenate(parts, axis=0) for parts in zip(state_t, state_i, strict=True)],
+        jnp.concatenate([queries_t, queries_i], axis=0),
+        jnp.concatenate([pos2, pos2_i], axis=0),
+        jnp.concatenate([low2, low2_i], axis=0),
+        kibuf[0].reshape(1024, HD),
+        kibuf[1].reshape(1024, HD),
+        ipos_live,
+    )
     result = (state[2] / state[1]).astype(BF)
     for g in range(2):
         placed = nn(place, result[256 + 32 * g : 288 + 32 * g])
         mixed = jnp.where(is_image, placed, result[128 * g : 128 * g + 128].astype(F32))
         out[:, 128 * g : 128 * g + 128] = mixed.astype(BF)
 
-    for cp in x1 + [vo_cp] + res_cp + w_cp + t_cp + rs_cp + ag_cp + y_cp + p4_cp:
+    for cp in x1 + [vo_cp] + res_cp + w_cp + list(t_cp.values()) + rs_cp + ag_cp + y_cp + p4_cp:
         cp.wait_send()
     for cp in (t_fwd, ag_fwd, p4_fwd, kv_fwd, ki_fwd):
         cp.wait_send()
@@ -408,31 +430,42 @@
     freq = np.power(np.float64(rope_base), exponent).astype(np.float32)
     freq = jnp.asarray(np.concatenate([freq, freq])[None, :])
     vm = pl.BlockSpec(memory_space=pltpu.VMEM)
-    hbm = pl.BlockSpec(memory_space=pl.ANY)
-    sm = pl.BlockSpec(memory_space=pltpu.SMEM)
     dma = pltpu.SemaphoreType.DMA
     args = [
-        (patch_rows, vm),
-        (vit_gain.reshape(1, VD), vm),
-        (vit_bias.reshape(1, VD), vm),
-        (jnp.transpose(vit_qkv, (1, 2, 3, 0)).reshape(3 * VHD, VD), vm),
-        (vit_out.reshape(VHD, VD), hbm),
-        (merge_gain.reshape(1, VD), vm),
-        (merge_bias.reshape(1, VD), vm),
-        (merge_weight, hbm),
-        (jnp.transpose(image_patches), vm),
-        (window_ids.reshape(1, 128), vm),
-        (image_pos.reshape(1, 1024), vm),
-        (slice_order, sm),
-        (slice_order.reshape(1, NC), vm),
-        (doc_ids.reshape(1, 4096), vm),
-        (text_rows, hbm),
-        (norm_gain.reshape(1, D), vm),
-        (w_query.reshape(2 * D, HD), hbm),
-        (w_keyval.reshape(D, HD), hbm),
-        (freq, vm),
+        patch_rows,
+        vit_gain,
+        vit_bias,
+        jnp.transpose(vit_qkv, (1, 2, 3, 0)).reshape(3 * VHD, VD),
+        vit_out.reshape(VHD, VD),
+        merge_gain,
+        merge_bias,
+        merge_weight,
+        jnp.transpose(image_patches),
+        window_ids.reshape(1, 128),
+        image_pos.reshape(1, 1024),
+        slice_order.reshape(1, NC),
+        doc_ids.reshape(1, 4096),
+        text_rows,
+        norm_gain.reshape(1, D),
+        w_query.reshape(2 * D, HD),
+        w_keyval.reshape(D, HD),
+        freq,
     ]
     scratch = [
+        pltpu.VMEM((128, VD), BF),
+        pltpu.VMEM((VD,), F32),
+        pltpu.VMEM((VD,), F32),
+        pltpu.VMEM((3 * VHD, VD), BF),
+        pltpu.VMEM((VD,), F32),
+        pltpu.VMEM((VD,), F32),
+        pltpu.VMEM((2, NC), jnp.int32),
+        pltpu.VMEM((1, 128), jnp.int32),
+        pltpu.VMEM((1, 1024), jnp.int32),
+        pltpu.SMEM((1, NC), jnp.int32),
+        pltpu.VMEM((1, NC), jnp.int32),
+        pltpu.VMEM((1, 4096), jnp.int32),
+        pltpu.VMEM((1, D), F32),
+        pltpu.VMEM((1, HD), F32),
         pltpu.VMEM((2 * D, HD), BF),
         pltpu.VMEM((D, 2 * HD), BF),
         pltpu.VMEM((D, HD), BF),
@@ -455,8 +488,8 @@
         pltpu.VMEM((32, D), BF),
         pltpu.VMEM((NC, 1, 256), F32),
         pltpu.VMEM((NC, 1, 256), F32),
-        pltpu.VMEM((1, 4096), F32),
-        dma((5,)),
+        pltpu.VMEM((4, 1, 1024), F32),
+        dma((19,)),
         dma((8,)), dma((8,)),
         dma, dma,
         dma((NX,)), dma((NX,)),
@@ -475,13 +508,13 @@
         kernel,
         name="fused",
         out_shape=jax.ShapeDtypeStruct((TOK, 256), BF),
-        in_specs=[spec for _, spec in args],
+        in_specs=[pl.BlockSpec(memory_space=pl.ANY)] * len(args),
         out_specs=vm,
         scratch_shapes=scratch,
         compiler_params=pltpu.CompilerParams(
-            collective_id=0, has_side_effects=True, vmem_limit_bytes=48 << 20
+            collective_id=0, has_side_effects=True, vmem_limit_bytes=63 << 20
         ),
-    )(*[value for value, _ in args])
+    )(*args)
     return result.reshape(TOK, 1, 256)
 
 

time: 101 us -> 78.5 us (0.78)
  local copies, waits for them, and re-layouts: 15.7 us -> 1.47 us
  Pallas kernels: 84.2 us -> 76.8 us
    unnamed x29 -> x1, local copies, waits for them, and re-layouts: 12.9 us -> 1.47 us
    pallas_call x1, Pallas kernels: 84.2 us -> 76.8 us  [local(): pl.pallas_call(kernel, name='fused', out_shape=jax.ShapeDtypeStruct((TOK,...]
    reshape x4 -> x0, local copies, waits for them, and re-layouts: 2.8 us -> none  [the longest x1 0.7 us: local(): vit_gain.reshape(1, VD)]
where the time goes in v2:
time: 78.5 us; the launch traced here: 78.3 us
  Pallas kernels  76.8 us (98%)
  local copies, waits for them, and re-layouts  1.47 us (2%)
    pallas_call x1, Pallas kernels, local(): pl.pallas_call(kernel, name='fused', out_shape=jax.ShapeDtypeStruct((TOK,...  76.8 us

profile of v2, /device:TPU:1, one launch (start us, length us, event | category | flops | bytes accessed | tf_op | source)
XLA Modules:
  0.0 78.3 jit_solution(12273459883764667587)
XLA Ops:
  0.0 76.8 %fused.1 = bf16[128,256]{1,0:T(8,128)(2,1)} custom-call(bf16[128,1280]{1,0:T(8,128)(2,1)} %patch_h.1, f32[1280]{0:T(1024)} %vgain_h.1, f32[1280]{0:T(1024)} %vbias_h.1, bf16[240,1280]{1,0:T(8,128)(2,1)} %bitcast.15, bf16[80,1280]{1,0:T(8,128)(2,1)} %bitcast.17, f32[1280]{0:T(1024)} %mgain_h.1, f32[1280]{0:T(1024)} %mbias_h.1, bf16[160,256]{1,0:T(8,128)(2,1)} %wblk.1, ...), custom_call_target="tpu_custom_call" | custom-call | tf_op jit(solution)/shard_map/fused/pallas_call | solution.py:507
  76.8 1.5 %copy.20 = bf16[128,1,256]{2,0,1:T(8,128)(2,1)} copy(bf16[128,1,256]{2,0,1:T(8,128)(2,1)} %bitcast.16) | data formatting | bytes 131072

commit v3 on v2

--- a/solution.py
+++ b/solution.py
@@ -161,9 +161,12 @@
     for k in range(1, NX):
         res_cp.append(remote(pp.at[lax.rem(x + k, NX) * 2 + t], res.at[x], ress.at[k], resr.at[k], at_x(k, t)))
         res_cp[-1].start()
-    t_cp = {
-        k: remote(tbuf.at[t, v], tbuf.at[t, v], ts.at[k], tr.at[k], at_v(k)) for k in range(1, NV)
-    }
+    def t_copy(block, k, sem):
+        blk = tbuf.at[t, lax.rem(v + block, NV)]
+        return remote(blk, blk, ts.at[sem], tr.at[sem], at_v(k))
+
+    t_cp = {k: t_copy(0, k, k) for k in (1, 7, 2, 6)}
+    t_cp.update({3: t_copy(6, 1, 3), 5: t_copy(2, 7, 5), 4: t_copy(6, 2, 4)})
     for k in (1, 7, 2, 6):
         t_cp[k].start()
     w_cp = [remote(wbuf.at[y], wbuf.at[y], ws.at[k], wr.at[k], at_y(k)) for k in range(1, NY)]
@@ -185,6 +188,8 @@
         cp.start()
         rs_cp.append(cp)
     rs_buf[v] = rs_src[v]
+    t_cp[2].wait_recv()
+    t_cp[6].wait_recv()
     for k in (3, 5, 4):
         t_cp[k].start()
 
@@ -273,7 +278,7 @@
     for cp in ag_cp:
         cp.start()
 
-    for k in range(1, NV):
+    for k in (1, 7, 3, 5, 4):
         t_cp[k].wait_recv()
     t_fwd = remote(tbuf.at[t], tbuf.at[t], fs.at[0], fr.at[0], partner)
     t_fwd.start()
@@ -282,10 +287,10 @@
     def normalise(buf, dst, rows):
         def squares(i, total):
             blk = buf[lax.rem(i, 2), i // 2].astype(F32)
-            return total + jnp.sum(blk * blk, axis=1, keepdims=True)
-
-        total = lax.fori_loop(0, 16, squares, jnp.zeros((rows, 1), F32))
-        scale = lax.rsqrt(total * (1.0 / D) + norm_eps)
+            return total + blk * blk
+
+        total = lax.fori_loop(0, 16, squares, jnp.zeros((rows, 256), F32))
+        scale = lax.rsqrt(jnp.sum(total, axis=1, keepdims=True) * (1.0 / D) + norm_eps)
         for i in range(16):
             cols = slice(256 * i, 256 * i + 256)
             dst[:, cols] = (buf[i % 2, i // 2].astype(F32) * scale * ngain[:, cols]).astype(BF)
@@ -294,10 +299,26 @@
     kv_t = nn(ntext[...], wkv[...])
     kvbuf[t, c] = jnp.where(t == 0, rotate(kv_t, cos_t, sin_t), kv_t).astype(BF)
 
-    def kv_copy(k):
-        return remote(kvbuf.at[t, c], kvbuf.at[t, c], kvs.at[k], kvr.at[k], at_c(k))
-
-    lax.fori_loop(1, NC, lambda k, z: (kv_copy(k).start(), z)[1], 0)
+    def along(buf, ss, rs):
+        def copy(n):
+            blk = buf.at[t, x * NY + lax.rem(y + lax.rem(n, NY), NY)] if n >= NY else buf.at[t, c]
+            d = at_x(n // NY, t) if n >= NY else at_y(n)
+            return remote(blk, blk, ss.at[n], rs.at[n], d)
+
+        return {n: copy(n) for n in range(1, NC)}
+
+    def send_own(copies):
+        for n in (1, 7, 2, 6, 3, 5, 4, 8, 24, 16):
+            copies[n].start()
+
+    def hand_on(copies, which):
+        for k in which:
+            copies[k].wait_recv()
+            for dx in (1, 3, 2):
+                copies[NY * dx + NY - k].start()
+
+    kv_cp = along(kvbuf, kvs, kvr)
+    send_own(kv_cp)
 
     for cp in ag_cp:
         cp.wait_recv()
@@ -320,6 +341,7 @@
         y_cp.append(cp)
     ybuf[x] = ysrc[x]
 
+    hand_on(kv_cp, (1, 7, 2, 6))
     for cp in y_cp:
         cp.wait_recv()
     emb = ybuf[0]
@@ -329,6 +351,7 @@
     p4_cp = [remote(p4.at[t, v], p4.at[t, v], p4s.at[k], p4r.at[k], at_v(k)) for k in range(1, NV)]
     for cp in p4_cp:
         cp.start()
+    hand_on(kv_cp, (3, 5, 4))
     q_t = nn(ntext[...], wq[...])
     q_t = [rotate(q_t[:, :128], cos_t, sin_t).astype(BF), rotate(q_t[:, 128:], cos_t, sin_t).astype(BF)]
 
@@ -338,6 +361,10 @@
     p4_fwd.start()
     p4_fwd.wait_recv()
     normalise(p4, nimg, 32)
+    kv_i = nn(nimg[...], wkv[...])
+    kibuf[t, c] = jnp.where(t == 0, rotate(kv_i, cos_i, sin_i), kv_i).astype(BF)
+    ki_cp = along(kibuf, kis, kir)
+    send_own(ki_cp)
     q_i = nn(nimg[...], wq[...])
     q_i = jnp.concatenate(
         [rotate(q_i[:, :128], cos_i, sin_i), rotate(q_i[:, 128:], cos_i, sin_i)], axis=1
@@ -350,16 +377,11 @@
     def q_copy(k):
         return remote(qsrc.at[lax.rem(c + k, NC)], qbuf.at[c], qs.at[k], qr.at[k], at_c(k))
 
-    kv_i = nn(nimg[...], wkv[...])
-    kibuf[t, c] = jnp.where(t == 0, rotate(kv_i, cos_i, sin_i), kv_i).astype(BF)
-
-    def ki_copy(k):
-        return remote(kibuf.at[t, c], kibuf.at[t, c], kis.at[k], kir.at[k], at_c(k))
-
-    lax.fori_loop(1, NC, lambda k, z: (ki_copy(k).start(), z)[1], 0)
     lax.fori_loop(1, NC, lambda k, z: (q_copy(k).start(), z)[1], 0)
-
-    lax.fori_loop(1, NC, lambda k, z: (kv_copy(k).wait_recv(), z)[1], 0)
+    hand_on(ki_cp, (1, 7, 2, 6, 3, 5, 4))
+
+    for n in range(NY, NC):
+        kv_cp[n].wait_recv()
     kv_fwd = remote(kvbuf.at[t], kvbuf.at[t], fs.at[3], fr.at[3], partner)
     kv_fwd.start()
     kv_fwd.wait_recv()
@@ -391,7 +413,8 @@
     pos2, low2 = jnp.concatenate([own_pos_f] * 2, axis=0), jnp.concatenate([low] * 2, axis=0)
     state_t = over_text(queries_t, pos2, low2)
 
-    lax.fori_loop(1, NC, lambda k, z: (ki_copy(k).wait_recv(), z)[1], 0)
+    for n in range(NY, NC):
+        ki_cp[n].wait_recv()
     ki_fwd = remote(kibuf.at[t], kibuf.at[t], fs.at[4], fr.at[4], partner)
     ki_fwd.start()
     lax.fori_loop(1, NC, lambda k, z: (q_copy(k).wait_recv(), z)[1], 0)
@@ -419,7 +442,10 @@
         cp.wait_send()
     for cp in (t_fwd, ag_fwd, p4_fwd, kv_fwd, ki_fwd):
         cp.wait_send()
-    lax.fori_loop(1, NC, lambda k, z: (kv_copy(k).wait_send(), ki_copy(k).wait_send(), q_copy(k).wait_send(), z)[3], 0)
+    for n in range(1, NC):
+        kv_cp[n].wait_send()
+        ki_cp[n].wait_send()
+    lax.fori_loop(1, NC, lambda k, z: (q_copy(k).wait_send(), z)[1], 0)
 
 
 def local(

time: 78.5 us -> 68.6 us (0.87)
  Pallas kernels: 76.8 us -> 67 us
    pallas_call x1, Pallas kernels: 76.8 us -> 67 us  [local(): pl.pallas_call(kernel, name='fused', out_shape=jax.ShapeDtypeStruct((TOK,...]
where the time goes in v3:
time: 68.6 us; the launch traced here: 68.5 us
  Pallas kernels  67 us (98%)
  local copies, waits for them, and re-layouts  1.47 us (2%)
    pallas_call x1, Pallas kernels, local(): pl.pallas_call(kernel, name='fused', out_shape=jax.ShapeDtypeStruct((TOK,...  67 us
    unnamed x1, local copies, waits for them, and re-layouts  1.47 us

profile of v3, /device:TPU:1, one launch (start us, length us, event | category | flops | bytes accessed | tf_op | source)
XLA Modules:
  0.0 68.5 jit_solution(16631021404795912733)
XLA Ops:
  0.0 67.0 %fused.1 = bf16[128,256]{1,0:T(8,128)(2,1)} custom-call(bf16[128,1280]{1,0:T(8,128)(2,1)} %patch_h.1, f32[1280]{0:T(1024)} %vgain_h.1, f32[1280]{0:T(1024)} %vbias_h.1, bf16[240,1280]{1,0:T(8,128)(2,1)} %bitcast.15, bf16[80,1280]{1,0:T(8,128)(2,1)} %bitcast.17, f32[1280]{0:T(1024)} %mgain_h.1, f32[1280]{0:T(1024)} %mbias_h.1, bf16[160,256]{1,0:T(8,128)(2,1)} %wblk.1, ...), custom_call_target="tpu_custom_call" | custom-call | tf_op jit(solution)/shard_map/fused/pallas_call | solution.py:533
  67.0 1.5 %copy.20 = bf16[128,1,256]{2,0,1:T(8,128)(2,1)} copy(bf16[128,1,256]{2,0,1:T(8,128)(2,1)} %bitcast.16) | data formatting | bytes 131072

commit v4 on v3

--- a/solution.py
+++ b/solution.py
@@ -71,9 +71,9 @@
     text, ngain_h, wq_raw, wkv_in, freq_h, out,
     patch, vgain, vbias, wqkv, mgain, mbias, ipatch, wids, ipos, sorder, sorder_v, docs, ngain, freq,
     wq_land, wq, wkv, wbuf, tbuf, ntext, kvbuf, kibuf, blp, mixb, vo, pp, res,
-    rs_src, rs_buf, ag, ysrc, ybuf, p4, nimg, qsrc, qbuf, kpos_s,
+    rs_src, rs_buf, ag, ysrc, ybuf, p4, nimg, n16, qsrc, qbuf, kpos_s,
     lsem, x1s, x1r, vos, vor, ress, resr, ws, wr, ts, tr, rss, rsr, ags, agr, ys, yr,
-    p4s, p4r, kvs, kvr, kis, kir, qs, qr, fs, fr,
+    p4s, p4r, kvs, kvr, kis, kir, qs, qr, fs, fr, tfs, tfr,
 ):
     v, c, t = lax.axis_index("vis"), lax.axis_index("ctx"), lax.axis_index("tp")
     x, y = c // NY, lax.rem(c, NY)
@@ -95,12 +95,12 @@
 
     pairs = [
         (patch_h, patch), (vgain_h, vgain), (vbias_h, vbias), (wqkv_h, wqkv), (wids_h, wids),
-        (vout, vo.at[t]), (text, tbuf.at[t, v]), (wblk, wbuf.at[y]),
+        (vout, vo.at[t]), (text, tbuf.at[t, v]), (wblk, wbuf.at[t, y]),
         (wq_raw, wq_land), (mgain_h, mgain), (mbias_h, mbias), (ipatch_h, ipatch), (ipos_h, ipos),
         (sorder_h, sorder_v), (sorder_h, sorder), (docs_h, docs), (ngain_h, ngain), (freq_h, freq), (wkv_in, wkv),
     ]
     loads = [pltpu.make_async_copy(a, b, lsem.at[n]) for n, (a, b) in enumerate(pairs)]
-    for load in loads:
+    for load in loads[:5]:
         load.start()
 
     barrier = pltpu.get_barrier_semaphore()
@@ -114,6 +114,8 @@
         greet(at_x(k, other))
     greet(partner)
     greetings = (NV - 1) + (NC - 1) + (NX - 1) + 1
+    for load in loads[5:]:
+        load.start()
 
 
     def remote(src, dst, ssem, rsem, d):
@@ -169,7 +171,7 @@
     t_cp.update({3: t_copy(6, 1, 3), 5: t_copy(2, 7, 5), 4: t_copy(6, 2, 4)})
     for k in (1, 7, 2, 6):
         t_cp[k].start()
-    w_cp = [remote(wbuf.at[y], wbuf.at[y], ws.at[k], wr.at[k], at_y(k)) for k in range(1, NY)]
+    w_cp = [remote(wbuf.at[t, y], wbuf.at[t, y], ws.at[k], wr.at[k], at_y(k)) for k in range(1, NY)]
     for cp in w_cp:
         cp.start()
     for cp in x1:
@@ -192,6 +194,16 @@
     t_cp[6].wait_recv()
     for k in (3, 5, 4):
         t_cp[k].start()
+
+    def t_other(k):
+        blk = tbuf.at[t, lax.rem(v + k, NV)]
+        return remote(blk, blk, tfs.at[k], tfr.at[k], partner)
+
+    t_fwd = [t_other(k) for k in range(NV)]
+    t_cp[1].wait_recv()
+    t_cp[7].wait_recv()
+    for k in (0, 1, 7, 2, 6):
+        t_fwd[k].start()
 
     for load in loads[8:]:
         load.wait()
@@ -273,29 +285,34 @@
         summed = summed + rs_buf[k].astype(F32)
     hidden = residual + unfold(summed)
     merged8 = layer_norm(hidden, mgain[...].reshape(1, VD), mbias[...].reshape(1, VD))
-    ag[t, v] = fold(merged8).astype(BF)
-    ag_cp = [remote(ag.at[t, v], ag.at[t, v], ags.at[k], agr.at[k], at_v(k)) for k in range(1, NV)]
+    ag[v] = fold(merged8).astype(BF)
+    ag_cp = [remote(ag.at[v], ag.at[v], ags.at[k], agr.at[k], at_v(k)) for k in range(1, NV)]
     for cp in ag_cp:
         cp.start()
 
-    for k in (1, 7, 3, 5, 4):
+    for cp in w_cp:
+        cp.wait_recv()
+    w_fwd = remote(wbuf.at[t], wbuf.at[t], fs.at[1], fr.at[1], partner)
+    w_fwd.start()
+
+    for k in (3, 5, 4):
         t_cp[k].wait_recv()
-    t_fwd = remote(tbuf.at[t], tbuf.at[t], fs.at[0], fr.at[0], partner)
-    t_fwd.start()
-    t_fwd.wait_recv()
+        t_fwd[NV - k].start()
+    for k in range(NV):
+        t_fwd[k].wait_recv()
 
     def normalise(buf, dst, rows):
         def squares(i, total):
-            blk = buf[lax.rem(i, 2), i // 2].astype(F32)
+            blk = buf(lax.rem(i, 2), i // 2).astype(F32)
             return total + blk * blk
 
         total = lax.fori_loop(0, 16, squares, jnp.zeros((rows, 256), F32))
         scale = lax.rsqrt(jnp.sum(total, axis=1, keepdims=True) * (1.0 / D) + norm_eps)
         for i in range(16):
             cols = slice(256 * i, 256 * i + 256)
-            dst[:, cols] = (buf[i % 2, i // 2].astype(F32) * scale * ngain[:, cols]).astype(BF)
-
-    normalise(tbuf, ntext, TOK)
+            dst[:, cols] = (buf(i % 2, i // 2).astype(F32) * scale * ngain[:, cols]).astype(BF)
+
+    normalise(lambda a, b: tbuf[a, b], ntext, TOK)
     kv_t = nn(ntext[...], wkv[...])
     kvbuf[t, c] = jnp.where(t == 0, rotate(kv_t, cos_t, sin_t), kv_t).astype(BF)
 
@@ -322,18 +339,15 @@
 
     for cp in ag_cp:
         cp.wait_recv()
-    ag_fwd = remote(ag.at[t], ag.at[t], fs.at[1], fr.at[1], partner)
-    ag_fwd.start()
-    for cp in w_cp:
-        cp.wait_recv()
-    ag_fwd.wait_recv()
-    half_of, rest = r256 // 128, lax.rem(r256, 128)
-    xs, j = rest // 32, lax.rem(rest, 32)
-    perm3 = hot(c256 == (j // 16) * 128 + (lax.rem(j, 16) // 2) * 16 + half_of * 8 + xs * 2 + lax.rem(j, 2))
-    mp = nn(perm3, ag[...].reshape(256, 640)).astype(BF)
-    wg = wbuf[...].reshape(VD, 256)
-    yv = nn(mp[:128], wg[:640]) + nn(mp[128:], wg[640:])
-    ysrc[...] = yv.reshape(NX, 32, 256)
+    w_fwd.wait_recv()
+    r128, c128 = iota((128, 128), 0), iota((128, 128), 1)
+    half_of, xs, j = r128 // 64, lax.rem(r128, 64) // 16, lax.rem(r128, 16)
+    perm3 = hot(c128 == (j // 2) * 16 + half_of * 8 + xs * 2 + lax.rem(j, 2))
+    mp = nn(perm3, ag[...].reshape(128, 640)).astype(BF)
+    for tt in range(NT):
+        wg = wbuf[tt].reshape(VD, 256)
+        yv = nn(mp[:64], wg[:640]) + nn(mp[64:], wg[640:])
+        ysrc[:, tt] = yv.reshape(NX, 16, 256)
     y_cp = []
     for k in range(1, NX):
         cp = remote(ysrc.at[lax.rem(x + k, NX)], ybuf.at[x], ys.at[k], yr.at[k], at_x(k, t))
@@ -347,8 +361,8 @@
     emb = ybuf[0]
     for k in range(1, NX):
         emb = emb + ybuf[k]
-    p4[t, v] = emb.astype(BF)
-    p4_cp = [remote(p4.at[t, v], p4.at[t, v], p4s.at[k], p4r.at[k], at_v(k)) for k in range(1, NV)]
+    p4[v] = emb.astype(BF)
+    p4_cp = [remote(p4.at[v], p4.at[v], p4s.at[k], p4r.at[k], at_v(k)) for k in range(1, NV)]
     for cp in p4_cp:
         cp.start()
     hand_on(kv_cp, (3, 5, 4))
@@ -357,10 +371,12 @@
 
     for cp in p4_cp:
         cp.wait_recv()
-    p4_fwd = remote(p4.at[t], p4.at[t], fs.at[2], fr.at[2], partner)
+    own_rows = pl.ds(pl.multiple_of(16 * t, 16), 16)
+    normalise(lambda a, b: p4[b, a], n16, 16)
+    nimg[own_rows, :] = n16[...]
+    p4_fwd = remote(n16, nimg.at[own_rows, :], fs.at[2], fr.at[2], partner)
     p4_fwd.start()
     p4_fwd.wait_recv()
-    normalise(p4, nimg, 32)
     kv_i = nn(nimg[...], wkv[...])
     kibuf[t, c] = jnp.where(t == 0, rotate(kv_i, cos_i, sin_i), kv_i).astype(BF)
     ki_cp = along(kibuf, kis, kir)
@@ -378,12 +394,11 @@
         return remote(qsrc.at[lax.rem(c + k, NC)], qbuf.at[c], qs.at[k], qr.at[k], at_c(k))
 
     lax.fori_loop(1, NC, lambda k, z: (q_copy(k).start(), z)[1], 0)
-    hand_on(ki_cp, (1, 7, 2, 6, 3, 5, 4))
-
     for n in range(NY, NC):
         kv_cp[n].wait_recv()
     kv_fwd = remote(kvbuf.at[t], kvbuf.at[t], fs.at[3], fr.at[3], partner)
     kv_fwd.start()
+    hand_on(ki_cp, (1, 7, 2, 6))
     kv_fwd.wait_recv()
     scale = 1.0 / math.sqrt(HD)
 
@@ -397,21 +412,23 @@
         total = total * factor + jnp.sum(p, axis=1, keepdims=True)
         return new, total, acc * factor + nn(p.astype(BF), values)
 
-    def over_text(queries, qpos, qlow):
-        rows = queries.shape[0]
-        state = (jnp.full((rows, 1), big_negative, F32), jnp.zeros((rows, 1), F32), jnp.zeros((rows, HD), F32))
-
+    def empty(rows):
+        return jnp.full((rows, 1), big_negative, F32), jnp.zeros((rows, 1), F32), jnp.zeros((rows, HD), F32)
+
+    def over_text(state, queries, qpos, qlow, blocks):
         def block(b, state):
             at = pl.ds(b * 8, 8)
             keys = kvbuf[0, at].reshape(1024, HD)
             values = kvbuf[1, at].reshape(1024, HD)
             return attend(state, queries, qpos, qlow, keys, values, kpos_s[b])
 
-        return lax.fori_loop(0, 4, block, state)
+        return lax.fori_loop(*blocks, block, state)
 
     queries_t = jnp.concatenate(q_t, axis=0)
     pos2, low2 = jnp.concatenate([own_pos_f] * 2, axis=0), jnp.concatenate([low] * 2, axis=0)
-    state_t = over_text(queries_t, pos2, low2)
+    state_t = over_text(empty(256), queries_t, pos2, low2, (0, 2))
+    hand_on(ki_cp, (3, 5, 4))
+    state_t = over_text(state_t, queries_t, pos2, low2, (2, 4))
 
     for n in range(NY, NC):
         ki_cp[n].wait_recv()
@@ -421,7 +438,7 @@
     q_in = jnp.concatenate([qbuf[e] for e in range(NC)], axis=0).astype(BF)
     queries_i = jnp.concatenate([q_in[:, :128], q_in[:, 128:]], axis=0)
     pos2_i, low2_i = jnp.concatenate([pos_i] * 2, axis=0), jnp.concatenate([low_i] * 2, axis=0)
-    state_i = over_text(queries_i, pos2_i, low2_i)
+    state_i = over_text(empty(64), queries_i, pos2_i, low2_i, (0, 4))
     ki_fwd.wait_recv()
     state = attend(
         [jnp.concatenate(parts, axis=0) for parts in zip(state_t, state_i, strict=True)],
@@ -440,7 +457,7 @@
 
     for cp in x1 + [vo_cp] + res_cp + w_cp + list(t_cp.values()) + rs_cp + ag_cp + y_cp + p4_cp:
         cp.wait_send()
-    for cp in (t_fwd, ag_fwd, p4_fwd, kv_fwd, ki_fwd):
+    for cp in t_fwd + [w_fwd, p4_fwd, kv_fwd, ki_fwd]:
         cp.wait_send()
     for n in range(1, NC):
         kv_cp[n].wait_send()
@@ -495,7 +512,7 @@
         pltpu.VMEM((2 * D, HD), BF),
         pltpu.VMEM((D, 2 * HD), BF),
         pltpu.VMEM((D, HD), BF),
-        pltpu.VMEM((NY, 160, 256), BF),
+        pltpu.VMEM((NT, NY, 160, 256), BF),
         pltpu.VMEM((NT, NV, TOK, 256), BF),
         pltpu.VMEM((TOK, D), BF),
         pltpu.VMEM((NT, NC, TOK, HD), BF),
@@ -507,11 +524,12 @@
         pltpu.VMEM((NX, 16, VD), BF),
         pltpu.VMEM((NV, 16, 640), BF),
         pltpu.VMEM((NV, 16, 640), BF),
-        pltpu.VMEM((NT, NV, 16, 640), BF),
-        pltpu.VMEM((NX, 32, 256), F32),
-        pltpu.VMEM((NX, 32, 256), F32),
-        pltpu.VMEM((NT, NV, 32, 256), BF),
+        pltpu.VMEM((NV, 16, 640), BF),
+        pltpu.VMEM((NX, NT, 16, 256), F32),
+        pltpu.VMEM((NX, NT, 16, 256), F32),
+        pltpu.VMEM((NV, NT, 16, 256), BF),
         pltpu.VMEM((32, D), BF),
+        pltpu.VMEM((16, D), BF),
         pltpu.VMEM((NC, 1, 256), F32),
         pltpu.VMEM((NC, 1, 256), F32),
         pltpu.VMEM((4, 1, 1024), F32),
@@ -529,6 +547,7 @@
         dma((NC,)), dma((NC,)),
         dma((NC,)), dma((NC,)),
         dma((5,)), dma((5,)),
+        dma((NV,)), dma((NV,)),
     ]
     result = pl.pallas_call(
         kernel,

time: 68.6 us -> 68.2 us (level)
  no operation moved by 1% of the time
where the time goes in v4:
time: 68.2 us; the launch traced here: 68.1 us
  Pallas kernels  66.6 us (98%)
  local copies, waits for them, and re-layouts  1.47 us (2%)
    pallas_call x1, Pallas kernels, local(): pl.pallas_call(kernel, name='fused', out_shape=jax.ShapeDtypeStruct((TOK,...  66.6 us
    unnamed x1, local copies, waits for them, and re-layouts  1.47 us

profile of v4, /device:TPU:1, one launch (start us, length us, event | category | flops | bytes accessed | tf_op | source)
XLA Modules:
  0.0 68.1 jit_solution(7932015373459913250)
XLA Ops:
  0.0 66.6 %fused.1 = bf16[128,256]{1,0:T(8,128)(2,1)} custom-call(bf16[128,1280]{1,0:T(8,128)(2,1)} %patch_h.1, f32[1280]{0:T(1024)} %vgain_h.1, f32[1280]{0:T(1024)} %vbias_h.1, bf16[240,1280]{1,0:T(8,128)(2,1)} %bitcast.15, bf16[80,1280]{1,0:T(8,128)(2,1)} %bitcast.17, f32[1280]{0:T(1024)} %mgain_h.1, f32[1280]{0:T(1024)} %mbias_h.1, bf16[160,256]{1,0:T(8,128)(2,1)} %wblk.1, ...), custom_call_target="tpu_custom_call" | custom-call | tf_op jit(solution)/shard_map/fused/pallas_call | solution.py:552
  66.6 1.5 %copy.20 = bf16[128,1,256]{2,0,1:T(8,128)(2,1)} copy(bf16[128,1,256]{2,0,1:T(8,128)(2,1)} %bitcast.16) | data formatting | bytes 131072
